TPU v7x, 32 devices: a whole 2x2x4 slice. The times are simulated.
32 devices in a mesh: dp: 16 (over z, y, x), fsdp: 2 (over core).
Axes of the slice: x: 2, y: 2, z: 4, core: 2. Of those that a mesh axis runs over, the one named last changes fastest.
Arguments:
- clean_images: float32 [128, 3, 1024], P(('dp', 'fsdp')), may hold values from -1 to 1
- noise_field: float32 [128, 3, 1024], P(('dp', 'fsdp')), may hold values from -6 to 6
- step_counts: int32 [128], P(('dp', 'fsdp')), may hold values from 2 to 4, as said below
- time_index: int32 [128], P(('dp', 'fsdp')), may hold values from 0 to 3
- teacher_size: int32 [128], P(('dp', 'fsdp')), may hold values from 1 to 2
- image_counts: int32 [32], P(('dp', 'fsdp')), may hold values from 2 to 4, as said below
- adam_step: int32 [1], replicated, may hold values from 2 to 20
- stem_master: float32 [327680], P(('dp', 'fsdp'))
- stem_first: float32 [327680], P(('dp', 'fsdp'))
- stem_second: float32 [327680], P(('dp', 'fsdp'))
- res_master: float32 [1409024], P(('dp', 'fsdp'))
- res_first: float32 [1409024], P(('dp', 'fsdp'))
- res_second: float32 [1409024], P(('dp', 'fsdp'))
- attn_master: float32 [294912], P(('dp', 'fsdp'))
- attn_first: float32 [294912], P(('dp', 'fsdp'))
- attn_second: float32 [294912], P(('dp', 'fsdp'))
- head_master: float32 [327680], P(('dp', 'fsdp'))
- head_first: float32 [327680], P(('dp', 'fsdp'))
- head_second: float32 [327680], P(('dp', 'fsdp'))
Outputs:
- loss_value: float32 [], replicated
- grad_norm: float32 [], replicated
- stem_master_out: float32 [327680], P(('dp', 'fsdp'))
- stem_first_out: float32 [327680], P(('dp', 'fsdp'))
- stem_second_out: float32 [327680], P(('dp', 'fsdp'))
- stem_copy_out: bfloat16 [327680], P(('dp', 'fsdp'))
- res_master_out: float32 [1409024], P(('dp', 'fsdp'))
- res_first_out: float32 [1409024], P(('dp', 'fsdp'))
- res_second_out: float32 [1409024], P(('dp', 'fsdp'))
- res_copy_out: bfloat16 [1409024], P(('dp', 'fsdp'))
- attn_master_out: float32 [294912], P(('dp', 'fsdp'))
- attn_first_out: float32 [294912], P(('dp', 'fsdp'))
- attn_second_out: float32 [294912], P(('dp', 'fsdp'))
- attn_copy_out: bfloat16 [294912], P(('dp', 'fsdp'))
- head_master_out: float32 [327680], P(('dp', 'fsdp'))
- head_first_out: float32 [327680], P(('dp', 'fsdp'))
- head_second_out: float32 [327680], P(('dp', 'fsdp'))
- head_copy_out: bfloat16 [327680], P(('dp', 'fsdp'))
Inputs may be any that keep to these rules, and one draw needn't show every extreme that they name: `step_counts`: each step count is 2 or 4. Device d's live images are its first image_counts[d] slots; some device has 4 live images and some has 2.
All inputs are finite; a program needn't handle non-finite values.
Results may differ from a plain program's by a relative error of at most 0.0091.
Values may be sent and summed in bfloat16 or wider, within the bound.
No kernel may reach another device: no remote copies, remote signals or barrier semaphores. Data moves between devices by JAX's collectives and lax.ppermute only.
A program may use at most 128 MiB of HBM per device.

v0:
```python
from functools import partial
import math

import jax
import jax.numpy as jnp
from jax import lax
from jax.experimental import pallas as pl
from jax.experimental.pallas import tpu as pltpu
from jax.sharding import PartitionSpec as P

C1 = 128
C2 = 256
GROUPS = 32
TDIM = 128
TEMB = 512
CIN = 3
SIDE = 32
LANES = 128
IMGS = 4
LOW = 256
ROWS = IMGS * LOW
PAD = 16
PADDED = LOW + 2 * PAD

clip_limit = 0.05
learn_rate = 0.05
beta_one = 0.9
beta_two = 0.999
adam_eps = 1e-08
decay_rate = 0.01
norm_eps = 1e-05

f32 = jnp.float32
bf16 = jnp.bfloat16
highest = lax.Precision.HIGHEST

STEM_ROWS, RES_ROWS, ATTN_ROWS, HEAD_ROWS = 2560, 11008, 2304, 2560

STEM_AT = dict(kern_in=0, bias_in=27, kern_down=28, bias_down=2332, end=2334)
RES_AT = dict(
    dense_one=0, bias_one=512, dense_two=516, bias_two=1540, gain_first=1542, shift_first=1544,
    kern_first=1546, bias_first=6154, gain_second=6156, shift_second=6158, kern_second=6160,
    bias_second=10768, end=10770,
)
ATTN_AT = dict(gain_attn=0, shift_attn=2, kern_qkv=4, kern_proj=1540, bias_proj=2052, end=2054)
HEAD_AT = dict(kern_up=0, bias_up=2304, gain_out=2305, shift_out=2306, kern_out=2307, bias_out=2334, end=2335)


def mm(a, b):
    return jnp.dot(a, b, preferred_element_type=f32)


def mm_nt(a, b):
    return lax.dot_general(a, b, (((1,), (1,)), ((), ())), preferred_element_type=f32)


def mm_tn(a, b):
    return lax.dot_general(a, b, (((0,), (0,)), ((), ())), preferred_element_type=f32)


def parts_of(values):
    high = values.astype(bf16)
    rest = values - high.astype(f32)
    middle = rest.astype(bf16)
    return high, middle, (rest - middle.astype(f32)).astype(bf16)


def mm_exact(values, matrix):
    return sum(mm(piece, matrix) for piece in parts_of(values))


def same_group(channels):
    size = channels // GROUPS
    down_at = lax.broadcasted_iota(jnp.int32, (channels, channels), 0) // size
    across = lax.broadcasted_iota(jnp.int32, (channels, channels), 1) // size
    return (down_at == across).astype(f32).astype(bf16)


def row_shift(values, step):
    count = values.shape[0]
    moved = pltpu.roll(values, (-step) % count, 0)
    column = lax.broadcasted_iota(jnp.int32, values.shape, 0) & 15
    return jnp.where(column == (0 if step < 0 else 15), 0.0, moved)


def chunks(total, size, body):
    def step(number, carry):
        body(pl.multiple_of(number * size, size))
        return carry

    lax.fori_loop(0, total // size, step, 0)


def widen(pieces, places, me, stage):
    for ref, (masks, lo, hi, per_shard, begin) in zip(pieces, places):
        for number, mask in enumerate(masks):
            owner = me ^ mask
            at = pl.multiple_of(owner * per_shard + begin, 8)
            stage[pl.ds(at, hi - lo), :] = ref[number, lo:hi, :].astype(f32)


def narrow_out(stage, me, outs, places):
    for ref, (masks, lo, hi, per_shard, begin) in zip(outs, places):
        for number, mask in enumerate(masks):
            owner = me ^ mask
            at = pl.multiple_of(owner * per_shard + begin, 8)
            ref[number, lo:hi, :] = stage[pl.ds(at, hi - lo), :].astype(ref.dtype)


def matrix_from(stage, base, out, depth, width):
    lanes = width // LANES

    def copy(at):
        for lane in range(lanes):
            out[pl.ds(at, 128), lane * LANES : (lane + 1) * LANES] = stage[
                pl.ds(base + lanes * at + lane, 128, lanes), :
            ].astype(bf16)

    chunks(depth, 128, copy)


def matrix_to(out, base, value):
    depth, width = value.shape
    lanes = width // LANES
    for lane in range(lanes):
        out[pl.ds(base + lane, depth, lanes), :] = value[:, lane * LANES : (lane + 1) * LANES]


def vector_at(stage, base, width):
    return jnp.concatenate([stage[base + lane : base + lane + 1, :] for lane in range(width // LANES)], axis=1)


def vector_to(out, base, value):
    for lane in range(value.shape[1] // LANES):
        out[base + lane : base + lane + 1, :] = value[:, lane * LANES : (lane + 1) * LANES]


def fold(values):
    return jnp.sum(values.reshape(values.shape[0] // 8, 8, values.shape[1]), axis=0)


def image_sums(load, phases, width):
    sums = []
    for image in range(IMGS):
        def step(number, carry):
            row = pl.multiple_of(image * LOW + number * 64, 64)
            for phase in range(phases):
                carry = tuple(c + fold(v) for c, v in zip(carry, load(phase, image, row)))
            return carry

        first = load(0, image, image * LOW)
        carry = lax.fori_loop(0, 4, step, tuple(jnp.zeros((8, width), f32) for _ in first))
        sums.append([jnp.sum(c, axis=0, keepdims=True) for c in carry])
    return [jnp.concatenate(list(group), axis=0) for group in zip(*sums)]


def norm_stats(load, phases, width, ones):
    count = LOW * phases * (width // GROUPS)
    (total,) = image_sums(lambda phase, image, row: (load(phase, row),), phases, width)
    center = mm_exact(total, ones) * (1.0 / count)

    def squares(phase, image, row):
        away = load(phase, row) - center[image : image + 1, :]
        return (away * away,)

    (total,) = image_sums(squares, phases, width)
    spread = mm_exact(total, ones) * (1.0 / count)
    return center, lax.rsqrt(spread + norm_eps)


def norm_back_stats(load, phases, width, gain, ones):
    count = LOW * phases * (width // GROUPS)
    shift_sum, gain_sum = image_sums(load, phases, width)
    means = mm_exact(jnp.concatenate([shift_sum * gain, gain_sum * gain], axis=0), ones) * (1.0 / count)
    return (
        jnp.sum(gain_sum, axis=0, keepdims=True),
        jnp.sum(shift_sum, axis=0, keepdims=True),
        means[:IMGS],
        means[IMGS:],
    )


def logistic(values):
    return 1.0 / (1.0 + jnp.exp(-values))


def each_chunk(body, phases=1, size=64):
    for image in range(IMGS):
        def step(number, carry):
            inside = pl.multiple_of(number * size, size)
            for phase in range(phases):
                body(phase, image, inside, image * LOW + inside)
            return carry

        lax.fori_loop(0, LOW // size, step, 0)


def clear_edges(wide):
    for image in range(IMGS):
        wide[image, 0:PAD, :] = jnp.zeros((PAD, wide.shape[2]), wide.dtype)
        wide[image, PAD + LOW : PADDED, :] = jnp.zeros((PAD, wide.shape[2]), wide.dtype)


def put_shifted(wide, image, inside, value):
    width = value.shape[1]
    at = pl.ds(PAD + inside, value.shape[0])
    wide[image, at, 0:width] = row_shift(value, -1).astype(bf16)
    wide[image, at, width : 2 * width] = value.astype(bf16)
    wide[image, at, 2 * width : 3 * width] = row_shift(value, 1).astype(bf16)


def wide_rows(wide, row_off, lo, hi):
    begin = PAD + 16 * row_off
    return wide[:, begin : begin + LOW, lo:hi].reshape(ROWS, hi - lo)


def conv_low(wide, kern):
    width = wide.shape[2]
    total = None
    for tap in range(3):
        part = mm(wide_rows(wide, tap - 1, 0, width), kern[tap * width : (tap + 1) * width, :])
        total = part if total is None else total + part
    return total


def conv_low_back(wide, kern):
    width = wide.shape[2] // 3
    total = None
    for row_tap in range(3):
        for col_tap in range(3):
            tap = row_tap * 3 + col_tap
            part = mm_nt(
                wide_rows(wide, 1 - row_tap, (2 - col_tap) * width, (3 - col_tap) * width),
                kern[tap * C2 : (tap + 1) * C2, :],
            )
            total = part if total is None else total + part
    return total


def conv_low_grad(source, wide, out, base):
    for row_tap in range(3):
        product = mm_tn(source[...], wide_rows(wide, 1 - row_tap, 0, 3 * C2))
        for col_tap in range(3):
            tap = row_tap * 3 + col_tap
            matrix_to(out, base + tap * 2 * C2, product[:, (2 - col_tap) * C2 : (3 - col_tap) * C2])


def lane_masks(width):
    place = lax.broadcasted_iota(jnp.int32, (8, width), 1)
    row, column = (place >> 4) & 15, place & 15

    def valid(row_off, col_off):
        keep = None
        for at, off in ((row, row_off), (column, col_off)):
            if off:
                inside = at != (0 if off < 0 else 15)
                keep = inside if keep is None else keep & inside
        return keep

    return {(r, c): valid(r, c) for r in (-1, 0, 1) for c in (-1, 0, 1)}


def lane_shift(values, row_off, col_off, masks):
    step = 16 * row_off + col_off
    if step == 0:
        return values
    moved = pltpu.roll(values, (-step) % values.shape[1], 1)
    return jnp.where(masks[(row_off, col_off)], moved, 0.0)


def tap_source(phase, tap_off):
    row, col = phase // 2 + tap_off[0], phase % 2 + tap_off[1]
    return (row % 2) * 2 + col % 2, row // 2, col // 2


TAPS = tuple((row - 1, col - 1) for row in range(3) for col in range(3))


def taps_on_lanes(source, out, masks, sign):
    for phase in range(4):
        for tap, off in enumerate(TAPS):
            other, row_off, col_off = tap_source(phase, (sign * off[0], sign * off[1]))
            out[8 * tap : 8 * tap + 8, phase * ROWS : (phase + 1) * ROWS] = lane_shift(
                source[:, other * ROWS : (other + 1) * ROWS], row_off, col_off, masks
            )


def down_wide(load, wide_one, wide_zero):
    clear_edges(wide_one)

    def body(phase, image, inside, row):
        at = pl.ds(PAD + inside, 64)
        for wide, row_phase in ((wide_one, 1), (wide_zero, 0)):
            right = load(row_phase * 2 + 1, row)
            left = load(row_phase * 2, row)
            wide[image, at, 0:C1] = row_shift(right, -1).astype(bf16)
            wide[image, at, C1 : 2 * C1] = left.astype(bf16)
            wide[image, at, 2 * C1 : 3 * C1] = right.astype(bf16)

    each_chunk(body)


def stem_forward(places, me, gathered, noisy, top, down, kern_down, stage, taps, wide_one, wide_zero):
    at = STEM_AT
    widen(gathered, places, me[0], stage)
    matrix_from(stage, at["kern_down"], kern_down, 9 * C1, C2)
    masks = lane_masks(ROWS)
    taps_on_lanes(noisy, taps, masks, 1)
    kern_in = jnp.concatenate(
        [
            jnp.concatenate([stage[3 * tap : 3 * tap + 3, :], jnp.zeros((5, LANES), f32)], axis=0)
            for tap in range(9)
        ],
        axis=0,
    ).astype(bf16)
    bias_in = stage[at["bias_in"] : at["bias_in"] + 1, :]
    for phase in range(4):
        top[phase] = mm_tn(taps[:, phase * ROWS : (phase + 1) * ROWS].astype(bf16), kern_in) + bias_in
    down_wide(lambda phase, row: top[phase, pl.ds(row, 64), :], wide_one, wide_zero)
    width = 3 * C1
    source = jnp.concatenate(
        [wide_rows(wide_one, -1, 0, width), wide_rows(wide_zero, 0, 0, width), wide_rows(wide_one, 0, 0, width)],
        axis=1,
    )
    down[...] = mm(source, kern_down[...]) + vector_at(stage, at["bias_down"], C2)


def stem_backward(leaving, me, noisy, top, skip, grad_down, kern_down, sent, out, taps, wide_one, wide_zero, wide_grad, low_grad):
    at = STEM_AT
    taps_on_lanes(noisy, taps, lane_masks(ROWS), 1)
    down_wide(lambda phase, row: top[phase, pl.ds(row, 64), :], wide_one, wide_zero)
    clear_edges(wide_grad)

    def body(phase, image, inside, row):
        value = grad_down[pl.ds(row, 64), :].astype(bf16).astype(f32)
        here = pl.ds(PAD + inside, 64)
        wide_grad[image, here, 0:C2] = value.astype(bf16)
        wide_grad[image, here, C2 : 2 * C2] = row_shift(value, 1).astype(bf16)

    each_chunk(body)
    bias_down = jnp.zeros((8, C2), f32)
    bias_down = lax.fori_loop(
        0,
        ROWS // 64,
        lambda n, c: c + fold(grad_down[pl.ds(pl.multiple_of(n * 64, 64), 64), :].astype(bf16).astype(f32)),
        bias_down,
    )
    vector_to(out, at["bias_down"], jnp.sum(bias_down, axis=0, keepdims=True))
    center = wide_rows(wide_grad, 0, 0, C2)
    width = 3 * C1
    for row_tap, (wide, row_off) in enumerate(((wide_one, -1), (wide_zero, 0), (wide_one, 0))):
        product = mm_tn(wide_rows(wide, row_off, 0, width), center)
        matrix_to(out, at["kern_down"] + row_tap * 2 * width, product)

    def taps_rows(first, count):
        return kern_down[first * C1 : (first + count) * C1, :]

    moved = wide_rows(wide_grad, 0, C2, 2 * C2)
    below = wide_rows(wide_grad, 1, 0, C2)
    below_moved = wide_rows(wide_grad, 1, C2, 2 * C2)
    first_pair = mm_nt(center, taps_rows(4, 2))
    second_pair = mm_nt(center, taps_rows(7, 2)) + mm_nt(below, taps_rows(1, 2))
    grads = (
        first_pair[:, :C1],
        first_pair[:, C1:] + mm_nt(moved, taps_rows(3, 1)),
        second_pair[:, :C1],
        second_pair[:, C1:] + mm_nt(moved, taps_rows(6, 1)) + mm_nt(below_moved, taps_rows(0, 1)),
    )
    bias_in = jnp.zeros((8, C1), f32)
    for phase in range(4):
        low_grad[phase] = (skip[phase] + grads[phase]).astype(bf16)
        bias_in = bias_in + fold(low_grad[phase].astype(f32))
    vector_to(out, at["bias_in"], jnp.sum(bias_in, axis=0, keepdims=True))
    kern_in = None
    for phase in range(4):
        part = mm(taps[:, phase * ROWS : (phase + 1) * ROWS].astype(bf16), low_grad[phase])
        kern_in = part if kern_in is None else kern_in + part
    for tap in range(9):
        out[3 * tap : 3 * tap + 3, :] = kern_in[8 * tap : 8 * tap + 3, :]
    out[at["end"] :, :] = jnp.zeros((STEM_ROWS - at["end"], LANES), f32)
    narrow_out(out, me[0], sent, leaving)


def res_forward(
    places, me, gathered, down, embed,
    inner, res_out, act_one, act_two, kern_first, kern_second, dense_two, hidden_pre, stats, gains,
    stage, dense_one, wide,
):
    at = RES_AT
    widen(gathered, places, me[0], stage)
    matrix_from(stage, at["dense_one"], dense_one, TDIM, TEMB)
    matrix_from(stage, at["dense_two"], dense_two, TEMB, C2)
    matrix_from(stage, at["kern_first"], kern_first, 9 * C2, C2)
    matrix_from(stage, at["kern_second"], kern_second, 9 * C2, C2)
    pre = jnp.dot(embed[...], dense_one[...].astype(f32), precision=highest) + vector_at(stage, at["bias_one"], TEMB)
    hidden_pre[...] = pre
    hidden = pre * logistic(pre)
    time_proj = jnp.dot(hidden, dense_two[...].astype(f32), precision=highest) + vector_at(stage, at["bias_two"], C2)
    ones = same_group(C2)
    clear_edges(wide)
    gain = vector_at(stage, at["gain_first"], C2)
    shift = vector_at(stage, at["shift_first"], C2)
    gain_two = vector_at(stage, at["gain_second"], C2)
    shift_two = vector_at(stage, at["shift_second"], C2)
    gains[...] = jnp.concatenate([gain, shift, gain_two, shift_two, jnp.zeros((4, C2), f32)], axis=0)

    def normalize(source, place, gain, shift, keep):
        center, scale = norm_stats(lambda phase, row: source[pl.ds(row, 64), :], 1, C2, ones)
        stats[place : place + IMGS, :] = center
        stats[place + IMGS : place + 2 * IMGS, :] = scale

        def body(phase, image, inside, row):
            value = (source[pl.ds(row, 64), :] - center[image : image + 1, :]) * scale[image : image + 1, :]
            value = value * gain + shift
            value = value * logistic(value)
            keep[pl.ds(row, 64), :] = value.astype(bf16)
            put_shifted(wide, image, inside, value.astype(bf16).astype(f32))

        each_chunk(body)

    normalize(down, 0, gain, shift, act_one)
    bias = vector_at(stage, at["bias_first"], C2)
    product = conv_low(wide, kern_first)
    for image in range(IMGS):
        inner[image * LOW : (image + 1) * LOW, :] = (
            product[image * LOW : (image + 1) * LOW, :] + bias + time_proj[image : image + 1, :]
        )
    normalize(inner, 2 * IMGS, gain_two, shift_two, act_two)
    res_out[...] = down[...] + conv_low(wide, kern_second) + vector_at(stage, at["bias_second"], C2)


def norm_back(load_grad, source, center, scale, gain, shift, ones, active, store):
    def pieces(image, row):
        xhat = (source[pl.ds(row, 64), :] - center[image : image + 1, :]) * scale[image : image + 1, :]
        grad = load_grad(row)
        if active:
            value = xhat * gain + shift
            gate = logistic(value)
            grad = grad * (gate * (1.0 + value * (1.0 - gate)))
        return grad, xhat

    def load(phase, image, row):
        grad, xhat = pieces(image, row)
        return grad, grad * xhat

    gain_grad, shift_grad, mean_one, mean_two = norm_back_stats(load, 1, C2, gain, ones)

    def body(phase, image, inside, row):
        grad, xhat = pieces(image, row)
        store(
            image,
            inside,
            row,
            scale[image : image + 1, :]
            * (grad * gain - mean_one[image : image + 1, :] - xhat * mean_two[image : image + 1, :]),
        )

    each_chunk(body)
    return gain_grad, shift_grad


def res_backward(
    leaving, me, grad_res, down, inner, act_one, act_two, kern_first, kern_second, dense_two, hidden_pre, stats, gains, embed,
    grad_down, sent, out,
    wide, grad_act,
):
    at = RES_AT
    ones = same_group(C2)
    clear_edges(wide)

    def lower(phase, image, inside, row):
        put_shifted(wide, image, inside, grad_res[pl.ds(row, 64), :].astype(bf16).astype(f32))

    each_chunk(lower)
    sums = image_sums(
        lambda phase, image, row: (grad_res[pl.ds(row, 64), :].astype(bf16).astype(f32),), 1, C2
    )[0]
    vector_to(out, at["bias_second"], jnp.sum(sums, axis=0, keepdims=True))
    grad_act[...] = conv_low_back(wide, kern_second)
    conv_low_grad(act_two, wide, out, at["kern_second"])

    def store_inner(image, inside, row, value):
        put_shifted(wide, image, inside, value.astype(bf16).astype(f32))

    gain_grad, shift_grad = norm_back(
        lambda row: grad_act[pl.ds(row, 64), :], inner, stats[8:12, :], stats[12:16, :],
        gains[2:3, :], gains[3:4, :], ones, True, store_inner,
    )
    vector_to(out, at["gain_second"], gain_grad)
    vector_to(out, at["shift_second"], shift_grad)
    inner_sum = jnp.concatenate(
        [
            jnp.sum(fold(wide[image, PAD : PAD + LOW, C2 : 2 * C2].astype(f32)), axis=0, keepdims=True)
            for image in range(IMGS)
        ]
        + [jnp.zeros((4, C2), f32)],
        axis=0,
    )
    time_sum = jnp.sum(inner_sum, axis=0, keepdims=True)
    vector_to(out, at["bias_first"], time_sum)
    vector_to(out, at["bias_two"], time_sum)
    pre = hidden_pre[...]
    gate = logistic(pre)
    contract = (((0,), (0,)), ((), ()))
    matrix_to(
        out, at["dense_two"],
        lax.dot_general(pre * gate, inner_sum, contract, precision=highest, preferred_element_type=f32),
    )
    grad_pre = lax.dot_general(
        inner_sum, dense_two[...].astype(f32), (((1,), (1,)), ((), ())), precision=highest, preferred_element_type=f32
    ) * (gate * (1.0 + pre * (1.0 - gate)))
    vector_to(out, at["bias_one"], jnp.sum(grad_pre, axis=0, keepdims=True))
    matrix_to(
        out, at["dense_one"],
        lax.dot_general(embed[...], grad_pre, contract, precision=highest, preferred_element_type=f32),
    )
    grad_act[...] = conv_low_back(wide, kern_first)
    conv_low_grad(act_one, wide, out, at["kern_first"])

    def store_down(image, inside, row, value):
        grad_down[pl.ds(row, 64), :] = value + grad_res[pl.ds(row, 64), :]

    gain_grad, shift_grad = norm_back(
        lambda row: grad_act[pl.ds(row, 64), :], down, stats[0:4, :], stats[4:8, :],
        gains[0:1, :], gains[1:2, :], ones, True, store_down,
    )
    vector_to(out, at["gain_first"], gain_grad)
    vector_to(out, at["shift_first"], shift_grad)
    out[at["end"] :, :] = jnp.zeros((RES_ROWS - at["end"], LANES), f32)
    narrow_out(out, me[0], sent, leaving)


def attn_forward(
    places, me, gathered, res_out,
    attn_low, normed, qkv, probs, mixed, kern_qkv, kern_proj, stats, gains,
    stage,
):
    at = ATTN_AT
    widen(gathered, places, me[0], stage)
    matrix_from(stage, at["kern_qkv"], kern_qkv, C2, 3 * C2)
    matrix_from(stage, at["kern_proj"], kern_proj, C2, C2)
    ones = same_group(C2)
    gain = vector_at(stage, at["gain_attn"], C2)
    shift = vector_at(stage, at["shift_attn"], C2)
    gains[...] = jnp.concatenate([gain, shift, jnp.zeros((6, C2), f32)], axis=0)
    center, scale = norm_stats(lambda phase, row: res_out[pl.ds(row, 64), :], 1, C2, ones)
    stats[0:IMGS, :] = center
    stats[IMGS : 2 * IMGS, :] = scale

    def body(phase, image, inside, row):
        value = (res_out[pl.ds(row, 64), :] - center[image : image + 1, :]) * scale[image : image + 1, :]
        normed[pl.ds(row, 64), :] = (value * gain + shift).astype(bf16)

    each_chunk(body)
    qkv[...] = mm(normed[...], kern_qkv[...]).astype(bf16)
    for image in range(IMGS):
        rows = slice(image * LOW, (image + 1) * LOW)
        logits = mm_nt(qkv[rows, 0:C2], qkv[rows, C2 : 2 * C2]) * C2 ** (-0.5)
        powers = jnp.exp(logits - jnp.max(logits, axis=1, keepdims=True))
        weights = powers / jnp.sum(powers, axis=1, keepdims=True)
        probs[image] = weights
        mixed[rows, :] = mm(weights.astype(bf16), qkv[rows, 2 * C2 : 3 * C2]).astype(bf16)
    attn_low[...] = (
        res_out[...] + mm(mixed[...], kern_proj[...]) + vector_at(stage, at["bias_proj"], C2)
    ).astype(bf16)


def attn_backward(
    leaving, me, grad_attn, res_out, normed, qkv, probs, mixed, kern_qkv, kern_proj, stats, gains,
    grad_res, sent, out,
    grad_qkv, grad_mixed, grad_normed, low,
):
    at = ATTN_AT
    ones = same_group(C2)
    low[...] = grad_attn[...].astype(bf16)
    sums = image_sums(lambda phase, image, row: (grad_attn[pl.ds(row, 64), :],), 1, C2)[0]
    vector_to(out, at["bias_proj"], jnp.sum(sums, axis=0, keepdims=True))
    matrix_to(out, at["kern_proj"], mm_tn(mixed[...], low[...]))
    grad_mixed[...] = mm_nt(low[...], kern_proj[...]).astype(bf16)
    scale_by = C2 ** (-0.5)
    for image in range(IMGS):
        rows = slice(image * LOW, (image + 1) * LOW)
        query, keys, value = (qkv[rows, part * C2 : (part + 1) * C2] for part in range(3))
        weights = probs[image]
        grad_probs = mm_nt(grad_mixed[rows, :], value)
        grad_qkv[rows, 2 * C2 : 3 * C2] = mm_tn(weights.astype(bf16), grad_mixed[rows, :]).astype(bf16)
        grad_logits = (
            weights * (grad_probs - jnp.sum(weights * grad_probs, axis=1, keepdims=True))
        ).astype(bf16)
        grad_qkv[rows, 0:C2] = (mm(grad_logits, keys) * scale_by).astype(bf16)
        grad_qkv[rows, C2 : 2 * C2] = (mm_tn(grad_logits, query) * scale_by).astype(bf16)
    matrix_to(out, at["kern_qkv"], mm_tn(normed[...], grad_qkv[...]))
    grad_normed[...] = mm_nt(grad_qkv[...], kern_qkv[...])

    def store(image, inside, row, value):
        grad_res[pl.ds(row, 64), :] = value + grad_attn[pl.ds(row, 64), :]

    gain_grad, shift_grad = norm_back(
        lambda row: grad_normed[pl.ds(row, 64), :], res_out, stats[0:4, :], stats[4:8, :],
        gains[0:1, :], gains[1:2, :], ones, False, store,
    )
    vector_to(out, at["gain_attn"], gain_grad)
    vector_to(out, at["shift_attn"], shift_grad)
    out[at["end"] :, :] = jnp.zeros((ATTN_ROWS - at["end"], LANES), f32)
    narrow_out(out, me[0], sent, leaving)


def pick(row, channel):
    lane = lax.broadcasted_iota(jnp.int32, (LANES, LANES), 0)
    ch = lax.broadcasted_iota(jnp.int32, (LANES, LANES), 1)
    return (row * LANES + lane == CIN * ch + channel).astype(f32).astype(bf16)


def head_step(
    places, leaving, me, gathered, attn_low, top, clean, factor,
    grad_attn, skip, loss, sent, out,
    stage, wide, kern_up, merged, act, taps, narrow, grad_wide_zero, grad_wide_one, boxes,
):
    at = HEAD_AT
    widen(gathered, places, me[0], stage)
    ones = same_group(C1)
    kern_up[...] = jnp.zeros(kern_up.shape, bf16)

    def combine(at_row):
        tap = [[stage[pl.ds((3 * a + b) * C2 + at_row, 64), :] for b in range(3)] for a in range(3)]
        by_row = {(0, 0): tap[0], (0, 1): [tap[1][b] + tap[2][b] for b in range(3)],
                  (1, 0): [tap[0][b] + tap[1][b] for b in range(3)], (1, 1): tap[2]}
        for (row_phase, slot), three in by_row.items():
            for col_off in range(3):
                base = (slot * 3 + col_off) * C2
                here = pl.ds(base + at_row, 64)
                if col_off == 0:
                    kern_up[row_phase, here, 0:C1] = three[0].astype(bf16)
                elif col_off == 1:
                    kern_up[row_phase, here, 0:C1] = (three[1] + three[2]).astype(bf16)
                    kern_up[row_phase, here, C1 : 2 * C1] = (three[0] + three[1]).astype(bf16)
                else:
                    kern_up[row_phase, here, C1 : 2 * C1] = three[2].astype(bf16)

    chunks(C2, 64, combine)
    clear_edges(wide)

    def spread_low(phase, image, inside, row):
        put_shifted(wide, image, inside, attn_low[pl.ds(row, 64), :].astype(f32))

    each_chunk(spread_low)
    bias_up = stage[at["bias_up"] : at["bias_up"] + 1, :]
    for row_phase in range(2):
        product = mm(
            jnp.concatenate(
                [wide_rows(wide, row_phase - 1, 0, 3 * C2), wide_rows(wide, row_phase, 0, 3 * C2)], axis=1
            ),
            kern_up[row_phase],
        )
        for col_phase in range(2):
            phase = row_phase * 2 + col_phase
            merged[phase] = product[:, col_phase * C1 : (col_phase + 1) * C1] + bias_up + top[phase]
    gain = stage[at["gain_out"] : at["gain_out"] + 1, :]
    shift = stage[at["shift_out"] : at["shift_out"] + 1, :]
    center, scale = norm_stats(lambda phase, row: merged[phase, pl.ds(row, 64), :], 4, C1, ones)

    def body(phase, image, inside, row):
        value = (merged[phase, pl.ds(row, 64), :] - center[image : image + 1, :]) * scale[image : image + 1, :]
        value = value * gain + shift
        act[phase, pl.ds(row, 64), :] = (value * logistic(value)).astype(bf16)

    each_chunk(body, 4)
    for channel in range(CIN):
        total = None
        for row in range(3):
            part = mm(stage[pl.ds(at["kern_out"] + row, 9, 3), :].astype(bf16), pick(row, channel))
            total = part if total is None else total + part
        narrow[pl.ds(channel, 9, 8), :] = total
    for channel in range(CIN, 8):
        narrow[pl.ds(channel, 9, 8), :] = jnp.zeros((9, LANES), f32)
    kern_out = narrow[...].astype(bf16)
    masks = lane_masks(ROWS)
    for phase in range(4):
        taps[:, phase * ROWS : (phase + 1) * ROWS] = mm_nt(kern_out, act[phase])
    lane = lax.broadcasted_iota(jnp.int32, (8, LANES), 1)
    channel_at = lax.broadcasted_iota(jnp.int32, (8, LANES), 0)
    bias_out = jnp.sum(
        jnp.where((lane == channel_at) & (channel_at < CIN), stage[at["bias_out"] : at["bias_out"] + 1, :], 0.0),
        axis=1,
        keepdims=True,
    )
    pixel_count = CIN * SIDE * SIDE
    loss_sum = jnp.zeros((8, ROWS), f32)
    bias_grad = jnp.zeros((8, 1), f32)
    grad_lanes = []
    for phase in range(4):
        predict = bias_out
        for tap, off in enumerate(TAPS):
            other, row_off, col_off = tap_source(phase, off)
            predict = predict + lane_shift(
                taps[8 * tap : 8 * tap + 8, other * ROWS : (other + 1) * ROWS], row_off, col_off, masks
            )
        error = predict - clean[:, phase * ROWS : (phase + 1) * ROWS]
        loss_sum = loss_sum + error * error * factor[...]
        grad = ((2.0 / pixel_count) * factor[...] * error).astype(bf16).astype(f32)
        bias_grad = bias_grad + jnp.sum(grad, axis=1, keepdims=True)
        grad_lanes.append(grad)
    loss[...] = jnp.sum(jnp.sum(loss_sum, axis=1, keepdims=True), axis=0, keepdims=True) * (1.0 / pixel_count)
    out[at["bias_out"] : at["bias_out"] + 1, :] = jnp.sum(
        jnp.where((lane == channel_at) & (channel_at < CIN), bias_grad, 0.0), axis=0, keepdims=True
    )
    for phase in range(4):
        for tap, off in enumerate(TAPS):
            other, row_off, col_off = tap_source(phase, (-off[0], -off[1]))
            taps[8 * tap : 8 * tap + 8, phase * ROWS : (phase + 1) * ROWS] = lane_shift(
                grad_lanes[other], row_off, col_off, masks
            )
    kern_grad = None
    for phase in range(4):
        low = taps[:, phase * ROWS : (phase + 1) * ROWS].astype(bf16)
        part = mm(low, act[phase])
        kern_grad = part if kern_grad is None else kern_grad + part
        skip[phase] = mm_tn(low, kern_out)
    narrow[...] = kern_grad
    for row in range(3):
        total = None
        for channel in range(CIN):
            pieces = parts_of(narrow[pl.ds(channel, 9, 8), :])
            part = sum(mm_nt(piece, pick(row, channel)) for piece in pieces)
            total = part if total is None else total + part
        out[pl.ds(at["kern_out"] + row, 9, 3), :] = total

    def pieces(phase, image, row):
        xhat = (merged[phase, pl.ds(row, 64), :] - center[image : image + 1, :]) * scale[image : image + 1, :]
        value = xhat * gain + shift
        gate = logistic(value)
        return skip[phase, pl.ds(row, 64), :] * (gate * (1.0 + value * (1.0 - gate))), xhat

    def load(phase, image, row):
        grad, xhat = pieces(phase, image, row)
        return grad, grad * xhat

    gain_grad, shift_grad, mean_one, mean_two = norm_back_stats(load, 4, C1, gain, ones)
    vector_to(out, at["gain_out"], gain_grad)
    vector_to(out, at["shift_out"], shift_grad)
    clear_edges(grad_wide_zero)
    clear_edges(grad_wide_one)
    clear_edges(boxes)
    wides = (grad_wide_zero, grad_wide_one)

    def back(phase, image, inside, row):
        for row_phase in range(2):
            pair = []
            for col_phase in range(2):
                phase = row_phase * 2 + col_phase
                grad, xhat = pieces(phase, image, row)
                value = scale[image : image + 1, :] * (
                    grad * gain - mean_one[image : image + 1, :] - xhat * mean_two[image : image + 1, :]
                )
                skip[phase, pl.ds(row, 64), :] = value
                pair.append(value.astype(bf16).astype(f32))
            put_shifted(wides[row_phase], image, inside, jnp.concatenate(pair, axis=1))
            here = pl.ds(PAD + inside, 64)
            base = row_phase * 3 * C1
            boxes[image, here, base : base + C1] = pair[1] + row_shift(pair[0], 1)
            boxes[image, here, base + C1 : base + 2 * C1] = pair[0] + pair[1]
            boxes[image, here, base + 2 * C1 : base + 3 * C1] = row_shift(pair[1], -1) + pair[0]

    each_chunk(back)
    bias_sum = jnp.zeros((8, C1), f32)
    for row_phase in range(2):
        for image in range(IMGS):
            both = fold(wides[row_phase][image, PAD : PAD + LOW, C2 : 2 * C2].astype(f32))
            bias_sum = bias_sum + both[:, :C1] + both[:, C1:]
    vector_to(out, at["bias_up"], jnp.sum(bias_sum, axis=0, keepdims=True))
    total = None
    for row_phase in range(2):
        for slot in range(2):
            row_off = row_phase - 1 + slot
            for col_off in range(3):
                part = mm_nt(
                    wide_rows(wides[row_phase], -row_off, (2 - col_off) * C2, (3 - col_off) * C2),
                    kern_up[row_phase, (slot * 3 + col_off) * C2 : (slot * 3 + col_off + 1) * C2, :],
                )
                total = part if total is None else total + part
    grad_attn[...] = total
    width = 3 * C1

    def box_rows(row_off, row_phase):
        return boxes[
            :, PAD + 16 * row_off : PAD + 16 * row_off + LOW, row_phase * width : (row_phase + 1) * width
        ].reshape(ROWS, width)

    summed = (
        box_rows(0, 1) + box_rows(1, 0),
        box_rows(0, 0) + box_rows(0, 1),
        box_rows(-1, 1) + box_rows(0, 0),
    )
    for row_tap in range(3):
        product = mm_tn(attn_low[...], summed[row_tap].astype(bf16))
        for col_tap in range(3):
            tap = row_tap * 3 + col_tap
            out[tap * C2 : (tap + 1) * C2, :] = product[:, col_tap * C1 : (col_tap + 1) * C1]
    out[at["end"] :, :] = jnp.zeros((HEAD_ROWS - at["end"], LANES), f32)
    narrow_out(out, me[0], sent, leaving)


def sds(shape, dtype=f32):
    return jax.ShapeDtypeStruct(shape, dtype)


def run(body, ins, outs, scratch):
    in_leaves, in_tree = jax.tree.flatten(ins)
    out_leaves, out_tree = jax.tree.flatten(outs)

    def kernel(*refs):
        split = len(in_leaves), len(in_leaves) + len(out_leaves)
        body(
            *jax.tree.unflatten(in_tree, refs[: split[0]]),
            *jax.tree.unflatten(out_tree, refs[split[0] : split[1]]),
            *refs[split[1] :],
        )

    whole = pl.BlockSpec(memory_space=pltpu.VMEM)
    results = pl.pallas_call(
        kernel,
        out_shape=out_leaves,
        in_specs=[pl.BlockSpec(memory_space=pltpu.SMEM)] + [whole] * (len(in_leaves) - 1),
        out_specs=[whole] * len(out_leaves),
        scratch_shapes=scratch,
        compiler_params=pltpu.CompilerParams(vmem_limit_bytes=52 * 2**20),
    )(*in_leaves)
    return jax.tree.unflatten(out_tree, results)


def wide_scratch(width, dtype=bf16):
    return pltpu.VMEM((IMGS, PADDED, width), dtype)


def forward_stem(me, weights, noisy):
    arrays, places = weights
    return run(
        partial(stem_forward, places),
        [me, arrays, noisy],
        [sds((4, ROWS, C1)), sds((ROWS, C2)), sds((9 * C1, C2), bf16)],
        [
            pltpu.VMEM((STEM_ROWS, LANES), f32), pltpu.VMEM((72, 4 * ROWS), f32),
            wide_scratch(3 * C1), wide_scratch(3 * C1),
        ],
    )


def forward_res(me, weights, down, embed):
    arrays, places = weights
    return run(
        partial(res_forward, places),
        [me, arrays, down, embed],
        [
            sds((ROWS, C2)), sds((ROWS, C2)), sds((ROWS, C2), bf16), sds((ROWS, C2), bf16),
            sds((9 * C2, C2), bf16), sds((9 * C2, C2), bf16), sds((TEMB, C2), bf16), sds((8, TEMB)),
            sds((16, C2)), sds((8, C2)),
        ],
        [pltpu.VMEM((RES_ROWS, LANES), f32), pltpu.VMEM((TDIM, TEMB), bf16), wide_scratch(3 * C2)],
    )


def forward_attn(me, weights, res_out):
    arrays, places = weights
    return run(
        partial(attn_forward, places),
        [me, arrays, res_out],
        [
            sds((ROWS, C2), bf16), sds((ROWS, C2), bf16), sds((ROWS, 3 * C2), bf16), sds((IMGS, LOW, LOW)),
            sds((ROWS, C2), bf16), sds((C2, 3 * C2), bf16), sds((C2, C2), bf16), sds((8, C2)), sds((8, C2)),
        ],
        [pltpu.VMEM((ATTN_ROWS, LANES), f32)],
    )


def both_head(me, weights, leaving, attn_low, top, clean, factor):
    arrays, places = weights
    shapes, out_places = leaving
    return run(
        partial(head_step, places, out_places),
        [me, arrays, attn_low, top, clean, factor],
        [sds((ROWS, C2)), sds((4, ROWS, C1)), sds((1, 1)), shapes],
        [
            pltpu.VMEM((HEAD_ROWS, LANES), f32),
            pltpu.VMEM((HEAD_ROWS, LANES), f32), wide_scratch(3 * C2), pltpu.VMEM((2, 6 * C2, C2), bf16),
            pltpu.VMEM((4, ROWS, C1), f32), pltpu.VMEM((4, ROWS, C1), bf16), pltpu.VMEM((72, 4 * ROWS), f32),
            pltpu.VMEM((72, LANES), f32), wide_scratch(3 * C2), wide_scratch(3 * C2), wide_scratch(6 * C1, f32),
        ],
    )


def backward_attn(me, leaving, *saved):
    shapes, out_places = leaving
    return run(
        partial(attn_backward, out_places),
        [me, *saved],
        [sds((ROWS, C2)), shapes],
        [
            pltpu.VMEM((ATTN_ROWS, LANES), f32),
            pltpu.VMEM((ROWS, 3 * C2), bf16), pltpu.VMEM((ROWS, C2), bf16), pltpu.VMEM((ROWS, C2), f32),
            pltpu.VMEM((ROWS, C2), bf16),
        ],
    )


def backward_res(me, leaving, *saved):
    shapes, out_places = leaving
    return run(
        partial(res_backward, out_places),
        [me, *saved],
        [sds((ROWS, C2)), shapes],
        [pltpu.VMEM((RES_ROWS, LANES), f32), wide_scratch(3 * C2), pltpu.VMEM((ROWS, C2), f32)],
    )


def backward_stem(me, leaving, *saved):
    shapes, out_places = leaving
    return run(
        partial(stem_backward, out_places),
        [me, *saved],
        [shapes],
        [
            pltpu.VMEM((STEM_ROWS, LANES), f32),
            pltpu.VMEM((72, 4 * ROWS), f32), wide_scratch(3 * C1), wide_scratch(3 * C1), wide_scratch(2 * C2),
            pltpu.VMEM((4, ROWS, C1), bf16),
        ],
    )


def plan(step_counts, time_index, teacher_size):
    position = time_index % step_counts
    time_values = (2 * position + teacher_size).astype(f32) / (2 * step_counts).astype(f32)
    alpha_t = jnp.cos(0.5 * math.pi * time_values)
    sigma_t = jnp.sin(0.5 * math.pi * time_values)
    weight = jnp.maximum(alpha_t * alpha_t / (sigma_t * sigma_t), 1.0)
    return (time_values, alpha_t, sigma_t, weight)


def sinusoid(time_values):
    half_dim = TDIM // 2
    frequency = jnp.exp(-math.log(10000.0) * jnp.arange(half_dim, dtype=f32) / half_dim)
    angles = 1000.0 * time_values[:, None] * frequency[None, :]
    return jnp.concatenate([jnp.sin(angles), jnp.cos(angles)], axis=1)


def by_phase(images):
    split = images.reshape(IMGS, CIN, 16, 2, 16, 2).transpose(1, 3, 5, 0, 2, 4).reshape(CIN, 4 * ROWS)
    return jnp.pad(split, ((0, 8 - CIN), (0, 0)))


def prepare(clean_images, noise_field, step_counts, time_index, teacher_size, image_count, total_live):
    slot_count = clean_images.shape[0]
    time_values, alpha_t, sigma_t, weight = plan(step_counts, time_index, teacher_size)
    live_mask = (jnp.arange(slot_count, dtype=jnp.int32) < image_count).astype(f32)
    factor = live_mask * weight / total_live
    noisy = (alpha_t[:, None, None] * clean_images + sigma_t[:, None, None] * noise_field).astype(bf16).astype(f32)
    embed = jnp.pad(sinusoid(time_values), ((0, 8 - IMGS), (0, 0)))
    factor_lanes = jnp.repeat(factor, LOW)[None, :]
    return by_phase(noisy), by_phase(clean_images), factor_lanes, embed


AXES = ("dp", "fsdp")


def swap(values, mask):
    count = lax.axis_size(AXES)
    return lax.ppermute(values, AXES, [(here, here ^ mask) for here in range(count)])


def axis_rounds(count, swapped):
    bits = [1 << at for at in range(1, count.bit_length() - 1)]
    plane = bits[:2][::-1] if swapped else bits[:2]
    rest = bits[2:]
    return [[bit] for bit in plane], [rest[at : at + 2] for at in range(0, len(rest), 2)]


def spans(bits):
    return [sum(bit for place, bit in enumerate(bits) if number >> place & 1) for number in range(1 << len(bits))]


def gather(shard, swapped):
    count = lax.axis_size(AXES)
    plane, rest = axis_rounds(count, swapped)
    held, masks = shard[None], [0]
    for bits in rest + plane[::-1]:
        reach = spans(bits)[1:]
        arrived = [swap(held, mask) for mask in reach]
        held = jnp.concatenate([held] + arrived, axis=0)
        masks = masks + [mask ^ own for mask in reach for own in masks]
    return [held, swap(held, 1)], [masks, [mask ^ 1 for mask in masks]]


def reduce_masks(count, swapped):
    plane, rest = axis_rounds(count, swapped)
    order = [0]
    for bits in (rest[::-1] + plane[::-1]):
        order = [mask ^ own for mask in spans(bits) for own in order]
    return order


def reduce(kept, sent, swapped):
    count = lax.axis_size(AXES)
    plane, rest = axis_rounds(count, swapped)
    total = kept.astype(f32) + swap(sent, 1).astype(f32)
    for bits in plane + rest:
        reach = spans(bits)
        size = total.shape[0] // len(reach)
        arrived = [swap(total[size * at : size * (at + 1)].astype(bf16), mask) for at, mask in enumerate(reach) if at]
        total = total[:size]
        for piece in arrived:
            total = total + piece.astype(f32)
    return total[0]


BLOCK_ROWS = (STEM_ROWS, RES_ROWS, ATTN_ROWS, HEAD_ROWS)
GATHERS = (
    (((0, 0, 80), (1, 0, 200)), False),
    (((1, 200, 344), (3, 0, 80), (2, 0, 72)), True),
)
REDUCES = (
    ((0, 80, False),),
    ((0, 176, False), (176, 344, True)),
    ((0, 72, True),),
    ((0, 80, False),),
)


def ordered_weights(shards):
    found = []
    for shard, rows in zip(shards, BLOCK_ROWS):
        whole = lax.all_gather(shard.reshape(-1), AXES, axis=0, tiled=True).reshape(1, rows, LANES)
        found.append(([whole], [([0], 0, rows, 0, 0)]))
    return found


def gathered_weights(shards):
    found = [([], []) for _ in shards]
    for members, swapped in GATHERS:
        group = jnp.concatenate([shards[block][lo:hi] for block, lo, hi in members], axis=0)
        arrays, masks = gather(group, swapped)
        at = 0
        for block, lo, hi in members:
            for array, owners in zip(arrays, masks):
                found[block][0].append(array)
                found[block][1].append((owners, at, at + hi - lo, shards[block].shape[0], lo))
            at += hi - lo
    return found


def leaving_shapes(block, count, ordered):
    rows = BLOCK_ROWS[block]
    if ordered:
        return [sds((1, rows, LANES))], [([0], 0, rows, 0, 0)]
    shapes, places = [], []
    for lo, hi, swapped in REDUCES[block]:
        masks = reduce_masks(count, swapped)
        for core in (0, 1):
            shapes.append(sds((count // 2, hi - lo, LANES), bf16))
            places.append(([mask ^ core for mask in masks], 0, hi - lo, rows // count, lo))
    return shapes, places


def reduced(block, leaving, ordered):
    if ordered:
        return lax.psum_scatter(leaving[0].reshape(-1), AXES, scatter_dimension=0, tiled=True)
    parts = []
    for number, (lo, hi, swapped) in enumerate(REDUCES[block]):
        parts.append(reduce(leaving[2 * number], leaving[2 * number + 1], swapped))
    return jnp.concatenate(parts, axis=0).reshape(-1)


def scalar_sums(values):
    count = lax.axis_size(AXES)
    row = jnp.concatenate([value.reshape(1) for value in values] + [jnp.zeros((LANES - len(values),), f32)])
    sent = jnp.broadcast_to(row[None, None, :], (count, 1, LANES))
    arrived = lax.all_to_all(sent, AXES, 0, 0, tiled=True)
    total = jnp.sum(arrived, axis=(0, 1))
    return [total[at] for at in range(len(values))]


def adam_update(master, first, second, gradient, step_value):
    first_new = beta_one * first + (1.0 - beta_one) * gradient
    second_new = beta_two * second + (1.0 - beta_two) * gradient * gradient
    fix_one = 1.0 - jnp.power(jnp.float32(beta_one), step_value)
    fix_two = 1.0 - jnp.power(jnp.float32(beta_two), step_value)
    master_new = master - learn_rate * (
        first_new / fix_one / (jnp.sqrt(second_new / fix_two) + adam_eps) + decay_rate * master
    )
    return (master_new, first_new, second_new, master_new.astype(bf16))


def per_device(
    clean_images, noise_field, step_counts, time_index, teacher_size, image_counts, adam_step,
    stem_master, stem_first, stem_second, res_master, res_first, res_second,
    attn_master, attn_first, attn_second, head_master, head_first, head_second,
):
    masters = (stem_master, res_master, attn_master, head_master)
    firsts = (stem_first, res_first, attn_first, head_first)
    seconds = (stem_second, res_second, attn_second, head_second)
    count = lax.axis_size(AXES)
    ordered = count != 32
    me = lax.axis_index(AXES).astype(jnp.int32).reshape(1)
    shards = [master.astype(bf16).reshape(-1, LANES) for master in masters]
    weights = ordered_weights(shards) if ordered else gathered_weights(shards)
    leaving = [leaving_shapes(block, count, ordered) for block in range(4)]
    (total_live,) = scalar_sums([image_counts[0].astype(f32)])
    noisy, clean, factor, embed = prepare(
        clean_images, noise_field, step_counts, time_index, teacher_size, image_counts[0], total_live
    )
    top, down, kern_down = forward_stem(me, weights[0], noisy)
    inner, res_out, act_one, act_two, kern_first, kern_second, dense_two, hidden_pre, stats, gains = forward_res(
        me, weights[1], down, embed
    )
    attn_low, normed, qkv, probs, mixed, kern_qkv, kern_proj, attn_stats, attn_gains = forward_attn(
        me, weights[2], res_out
    )
    grad_attn, skip, loss_local, head_out = both_head(
        me, weights[3], leaving[3], attn_low, top, clean, factor
    )
    grad_res, attn_out = backward_attn(
        me, leaving[2], grad_attn, res_out, normed, qkv, probs, mixed, kern_qkv, kern_proj, attn_stats, attn_gains
    )
    grad_down, res_out_grads = backward_res(
        me, leaving[1], grad_res, down, inner, act_one, act_two, kern_first, kern_second, dense_two, hidden_pre,
        stats, gains, embed,
    )
    (stem_out,) = backward_stem(me, leaving[0], noisy, top, skip, grad_down, kern_down)
    shard_grads = [
        reduced(block, out, ordered) for block, out in enumerate((stem_out, res_out_grads, attn_out, head_out))
    ]
    sum_local = sum((jnp.sum(jnp.square(gradient)) for gradient in shard_grads))
    loss_value, sum_sq = scalar_sums([loss_local, sum_local])
    grad_norm = jnp.sqrt(sum_sq)
    clip_scale = clip_limit / jnp.maximum(grad_norm, clip_limit)
    step_value = adam_step[0].astype(f32)
    results = [loss_value, grad_norm]
    for block_idx in range(4):
        results.extend(
            adam_update(
                masters[block_idx], firsts[block_idx], seconds[block_idx], shard_grads[block_idx] * clip_scale, step_value
            )
        )
    return tuple(results)


def solution(mesh):
    split = P(("dp", "fsdp"))
    images = P(("dp", "fsdp"), None, None)
    return jax.shard_map(
        per_device,
        mesh=mesh,
        in_specs=(images, images, split, split, split, split, P()) + (split,) * 12,
        out_specs=(P(), P()) + (split,) * 16,
        check_vma=False,
    )
```

profile of v0, /device:TPU:0, one launch (start us, length us, event | category | flops | bytes accessed | tf_op | source)
XLA Modules:
  0.0 209.5 jit_solution(16165692755096724960)
XLA Ops:
  3.2 3.1 %collective-permute-start = (bf16[1,296,128]{2,1,0:T(8,128)(2,1)S(1)}, bf16[1,296,128]{2,1,0:T(8,128)(2,1)S(1)}, u32[]{:S(2)}, u32[]{:S(2)}) collective-permute-start(bf16[1,296,128]{2,1,0:T(8,128)(2,1)S(1)} %maximum_bitcast_fusion), channel_id=1, source_target_pairs={{0,8},{1,9},{2,10},{3,11},{4,12},{5,13},{6,14},{7,15},{8,0},{9,1},... | collective-permute-start | bytes 227336 | tf_op jit(solution)/shard_map/ppermute | solution.py:966
  6.3 2.6 %collective-permute-start.1 = (bf16[1,296,128]{2,1,0:T(8,128)(2,1)S(1)}, bf16[1,296,128]{2,1,0:T(8,128)(2,1)S(1)}, u32[]{:S(2)}, u32[]{:S(2)}) collective-permute-start(bf16[1,296,128]{2,1,0:T(8,128)(2,1)S(1)} %maximum_bitcast_fusion), channel_id=1, source_target_pairs={{0,16},{1,17},{2,18},{3,19},{4,20},{5,21},{6,22},{7,23},{8,24},{9,... | collective-permute-start | bytes 227336 | tf_op jit(solution)/shard_map/ppermute | solution.py:966
  10.2 3.9 %collective-permute-start.8 = (bf16[1,280,128]{2,1,0:T(8,128)(2,1)S(1)}, bf16[1,280,128]{2,1,0:T(8,128)(2,1)S(1)}, u32[]{:S(2)}, u32[]{:S(2)}) collective-permute-start(bf16[1,280,128]{2,1,0:T(8,128)(2,1)S(1)} %maximum_bitcast_fusion.1), channel_id=1, source_target_pairs={{0,24},{1,25},{2,26},{3,27},{4,28},{5,29},{6,30},{7,31},{8,16},{9,... | collective-permute-start | bytes 215048 | tf_op jit(solution)/shard_map/ppermute | solution.py:966
  15.4 2.8 %all-to-all-start = ((f32[32,1,128]{2,1,0:T(1,128)}), f32[32,1,128]{2,1,0:T(1,128)S(1)}, u32[]{:S(2)}, u32[]{:S(2)}) async-start(f32[32,1,128]{2,1,0:T(1,128)} %broadcast_in_dim.14), calls=%async_computation | async-start | bytes 32768 | tf_op jit(solution)/shard_map/all_to_all | solution.py:1075
  19.5 3.6 %collective-permute-start.2 = (bf16[1,296,128]{2,1,0:T(8,128)(2,1)S(1)}, bf16[1,296,128]{2,1,0:T(8,128)(2,1)S(1)}, u32[]{:S(2)}, u32[]{:S(2)}) collective-permute-start(bf16[1,296,128]{2,1,0:T(8,128)(2,1)S(1)} %maximum_bitcast_fusion), channel_id=1, source_target_pairs={{0,24},{1,25},{2,26},{3,27},{4,28},{5,29},{6,30},{7,31},{8,16},{9,... | collective-permute-start | bytes 227336 | tf_op jit(solution)/shard_map/ppermute | solution.py:966
  23.1 1.6 collective-permute-start.9
  26.7 1.5 collective-permute-start.3
  30.2 1.7 collective-permute-done.9
  32.6 1.5 collective-permute-start.10
  34.1 2.3 %collective-permute-done.3 = bf16[4,296,128]{2,1,0:T(8,128)(2,1)S(1)} collective-permute-done((bf16[4,296,128]{2,1,0:T(8,128)(2,1)S(1)}, bf16[4,296,128]{2,1,0:T(8,128)(2,1)S(1)}, u32[]{:S(2)}, u32[]{:S(2)}) %collective-permute-start.3) | collective-permute-done | bytes 303136 | tf_op jit(solution)/shard_map/ppermute | solution.py:966
  37.8 1.6 copy.50
  40.0 7.9 %collective-permute-done.10 = bf16[8,280,128]{2,1,0:T(8,128)(2,1)} collective-permute-done((bf16[8,280,128]{2,1,0:T(8,128)(2,1)}, bf16[8,280,128]{2,1,0:T(8,128)(2,1)}, u32[]{:S(2)}, u32[]{:S(2)}) %collective-permute-start.10) | collective-permute-done | bytes 573472 | tf_op jit(solution)/shard_map/ppermute | solution.py:966
  47.8 1.9 constant_dynamic-update-slice_fusion.16.refs_1_
  49.8 1.1 collective-permute-done.4
  50.8 1.1 constant_dynamic-update-slice_fusion.5.refs_3_.refs_1_
  52.6 1.6 copy.48
  54.8 4.3 %shard_map.322 = (f32[4,1024,128]{2,1,0:T(8,128)}, f32[1024,256]{1,0:T(8,128)S(1)}, bf16[1152,256]{1,0:T(8,128)(2,1)S(1)}) custom-call(s32[1]{0:T(128)} %bitcast.refs_0_, bf16[16,280,128]{2,1,0:T(8,128)(2,1)} %constant_dynamic-update-slice_fusion.16.refs_1_, bf16[16,280,128]{2,1,0:T(8,128)(2,1)} %collective-permute-done.11.refs_2_, ...), custom_call_target="tpu_custom_call" | custom-call | tf_op jit(solution)/shard_map/pallas_call | solution.py:820
  60.1 1.1 copy-done.2
  61.2 13.9 %shard_map.323 = (f32[1024,256]{1,0:T(8,128)}, f32[1024,256]{1,0:T(8,128)}, bf16[1024,256]{1,0:T(8,128)(2,1)S(1)}, bf16[1024,256]{1,0:T(8,128)(2,1)S(1)}, bf16[2...) custom-call(s32[1]{0:T(128)} %bitcast.refs_0_, ...), custom_call_target="tpu_custom_call" | custom-call | tf_op jit(solution)/shard_map/pallas_call | solution.py:820
  75.1 6.0 %shard_map.324 = (bf16[1024,256]{1,0:T(8,128)(2,1)S(1)}, bf16[1024,256]{1,0:T(8,128)(2,1)S(1)}, bf16[1024,768]{1,0:T(8,128)(2,1)}, f32[4,256,256]{2,1,0:T(8,128)...) custom-call(s32[1]{0:T(128)} %bitcast.refs_0_, ...), custom_call_target="tpu_custom_call" | custom-call | tf_op jit(solution)/shard_map/pallas_call | solution.py:820
  81.1 18.0 %shard_map.325 = (f32[1024,256]{1,0:T(8,128)}, f32[4,1024,128]{2,1,0:T(8,128)}, f32[1,1]{1,0:T(1,128)}, bf16[16,80,128]{2,1,0:T(8,128)(2,1)S(1)}, bf16[16,80,128]{2,1,0:T(8,128)(2,1)S(1)}) custom-call(s32[1]{0:T(128)} %bitcast.refs_0_, bf16[16,296,128]{2,1,0:T(8,128)(2,1)} %copy-done.1, bf16[16,296,128]{2,1,0:T(8,128)(2,1)} %copy-done.2, ...), custom_call_target="tpu_custom_call" | custom-call | tf_op jit(solution)/shard_map/pallas_call | solution.py:820
  99.0 7.1 %shard_map.326 = (f32[1024,256]{1,0:T(8,128)}, bf16[16,72,128]{2,1,0:T(8,128)(2,1)S(1)}, bf16[16,72,128]{2,1,0:T(8,128)(2,1)S(1)}) custom-call(s32[1]{0:T(128)} %bitcast.refs_0_, f32[1024,256]{1,0:T(8,128)} %get-tuple-element.61.refs_1_, f32[1024,256]{1,0:T(8,128)} %get-tuple-element.56.refs_3_.refs_2_, bf16[1024,256]{1,0:T(8,128)(2,1)S(1)} %get-tuple-element.62.refs_3_, ...), custom_call_target="tpu_custom_call" | custom-call | tf_op jit(solution)/shard_map/pallas_call | solution.py:820
  106.7 15.8 %shard_map.327 = (f32[1024,256]{1,0:T(8,128)}, bf16[16,176,128]{2,1,0:T(8,128)(2,1)}, bf16[16,176,128]{2,1,0:T(8,128)(2,1)}, bf16[16,168,128]{2,1,0:T(8,128)(2,1)}, bf16[16,168,128]{2,1,0:T(8,128)(2,1)}) custom-call(s32[1]{0:T(128)} %bitcast.refs_0_, f32[1024,256]{1,0:T(8,128)} %get-tuple-element.70.refs_1_, f32[1024,256]{1,0:T(8,128)} %copy-done, ...), custom_call_target="tpu_custom_call" | custom-call | tf_op jit(solution)/shard_map/pallas_call | solution.py:820
  123.0 5.4 %shard_map.328 = (bf16[16,80,128]{2,1,0:T(8,128)(2,1)S(1)}, bf16[16,80,128]{2,1,0:T(8,128)(2,1)S(1)}) custom-call(s32[1]{0:T(128)} %bitcast.refs_0_, f32[8,4096]{1,0:T(8,128)S(1)} %pad_convert_fusion.refs_3_.refs_1_, f32[4,1024,128]{2,1,0:T(8,128)} %get-tuple-element.58.refs_4_.refs_2_, f32[4,1024,128]{2,1,0:T(8,128)} %get-tuple-element.60.refs_3_, ...), custom_call_target="tpu_custom_call" | custom-call | tf_op jit(solution)/shard_map/pallas_call | solution.py:820
  129.5 1.5 collective-permute-start.37
  131.8 3.0 %collective-permute-done.31 = bf16[8,72,128]{2,1,0:T(8,128)(2,1)S(1)} collective-permute-done((bf16[8,72,128]{2,1,0:T(8,128)(2,1)S(1)}, bf16[8,72,128]{2,1,0:T(8,128)(2,1)S(1)}, u32[]{:S(2)}, u32[]{:S(2)}) %collective-permute-start.31) | collective-permute-done | bytes 147488 | tf_op jit(solution)/shard_map/ppermute | solution.py:966
  134.9 1.5 collective-permute-start.32
  136.7 3.8 %collective-permute-done.32 = bf16[4,72,128]{2,1,0:T(8,128)(2,1)S(1)} collective-permute-done((bf16[4,72,128]{2,1,0:T(8,128)(2,1)S(1)}, bf16[4,72,128]{2,1,0:T(8,128)(2,1)S(1)}, u32[]{:S(2)}, u32[]{:S(2)}) %collective-permute-start.32) | collective-permute-done | bytes 73760 | tf_op jit(solution)/shard_map/ppermute | solution.py:966
  140.8 3.0 %collective-permute-start.34 = (bf16[1,72,128]{2,1,0:T(8,128)(2,1)S(1)}, bf16[1,72,128]{2,1,0:T(8,128)(2,1)S(1)}, u32[]{:S(2)}, u32[]{:S(2)}) collective-permute-start(bf16[1,72,128]{2,1,0:T(8,128)(2,1)S(1)} %get-tuple-element.152), channel_id=1, source_target_pairs={{0,16},{1,17},{2,18},{3,19},{4,20},{5,21},{6,22},{7,23},{8,24},{9,... | collective-permute-start | bytes 55304 | tf_op jit(solution)/shard_map/ppermute | solution.py:966
  143.8 1.2 collective-permute-start.35
  145.1 1.8 collective-permute-start.38
  147.4 1.9 collective-permute-done.35
  150.1 2.8 %collective-permute-start.40 = (bf16[1,80,128]{2,1,0:T(8,128)(2,1)S(1)}, bf16[1,80,128]{2,1,0:T(8,128)(2,1)S(1)}, u32[]{:S(2)}, u32[]{:S(2)}) collective-permute-start(bf16[1,80,128]{2,1,0:T(8,128)(2,1)S(1)} %get-tuple-element.138), channel_id=1, source_target_pairs={{0,16},{1,17},{2,18},{3,19},{4,20},{5,21},{6,22},{7,23},{8,24},{9,... | collective-permute-start | bytes 61448 | tf_op jit(solution)/shard_map/ppermute | solution.py:966
  152.9 1.6 collective-permute-start.41
  155.0 2.6 %collective-permute-start.16 = (bf16[1,80,128]{2,1,0:T(8,128)(2,1)S(1)}, bf16[1,80,128]{2,1,0:T(8,128)(2,1)S(1)}, u32[]{:S(2)}, u32[]{:S(2)}) collective-permute-start(bf16[1,80,128]{2,1,0:T(8,128)(2,1)S(1)} %get-tuple-element.141), channel_id=1, source_target_pairs={{0,16},{1,17},{2,18},{3,19},{4,20},{5,21},{6,22},{7,23},{8,24},{9,... | collective-permute-start | bytes 61448 | tf_op jit(solution)/shard_map/ppermute | solution.py:966
  157.6 1.2 collective-permute-done.41
  158.7 1.3 collective-permute-start.17
  161.0 1.5 collective-permute-start.25
  162.8 1.5 collective-permute-start.19
  164.9 4.6 %collective-permute-done.25 = bf16[8,168,128]{2,1,0:T(8,128)(2,1)S(1)} collective-permute-done((bf16[8,168,128]{2,1,0:T(8,128)(2,1)S(1)}, bf16[8,168,128]{2,1,0:T(8,128)(2,1)S(1)}, u32[]{:S(2)}, u32[]{:S(2)}) %collective-permute-start.25) | collective-permute-done | bytes 344096 | tf_op jit(solution)/shard_map/ppermute | solution.py:966
  169.7 1.5 collective-permute-start.26
  171.3 2.2 %collective-permute-start.20 = (bf16[4,176,128]{2,1,0:T(8,128)(2,1)S(1)}, bf16[4,176,128]{2,1,0:T(8,128)(2,1)S(1)}, u32[]{:S(2)}, u32[]{:S(2)}) collective-permute-start(bf16[4,176,128]{2,1,0:T(8,128)(2,1)S(1)} %slice.324), channel_id=1, source_target_pairs={{0,4},{1,5},{2,6},{3,7},{4,0},{5,1},{6,2},{7,3},{8,12},{9,13},{10,... | collective-permute-start | bytes 540680 | tf_op jit(solution)/shard_map/ppermute | solution.py:966
  173.5 1.6 collective-permute-done.26
  175.3 3.7 %collective-permute-start.28 = (bf16[1,168,128]{2,1,0:T(8,128)(2,1)S(1)}, bf16[1,168,128]{2,1,0:T(8,128)(2,1)S(1)}, u32[]{:S(2)}, u32[]{:S(2)}) collective-permute-start(bf16[1,168,128]{2,1,0:T(8,128)(2,1)S(1)} %get-tuple-element.135), channel_id=1, source_target_pairs={{0,16},{1,17},{2,18},{3,19},{4,20},{5,21},{6,22},{7,23},{8,24},{9,... | collective-permute-start | bytes 129032 | tf_op jit(solution)/shard_map/ppermute | solution.py:966
  179.9 3.7 %collective-permute-start.22 = (bf16[1,176,128]{2,1,0:T(8,128)(2,1)S(1)}, bf16[1,176,128]{2,1,0:T(8,128)(2,1)S(1)}, u32[]{:S(2)}, u32[]{:S(2)}) collective-permute-start(bf16[1,176,128]{2,1,0:T(8,128)(2,1)S(1)} %get-tuple-element.132), channel_id=1, source_target_pairs={{0,16},{1,17},{2,18},{3,19},{4,20},{5,21},{6,22},{7,23},{8,24},{9,... | collective-permute-start | bytes 135176 | tf_op jit(solution)/shard_map/ppermute | solution.py:966
  185.6 3.8 %collective-permute-done.23 = bf16[1,176,128]{2,1,0:T(8,128)(2,1)S(1)} collective-permute-done((bf16[1,176,128]{2,1,0:T(8,128)(2,1)S(1)}, bf16[1,176,128]{2,1,0:T(8,128)(2,1)S(1)}, u32[]{:S(2)}, u32[]{:S(2)}) %collective-permute-start.23) | collective-permute-done | bytes 45088 | tf_op jit(solution)/shard_map/ppermute | solution.py:966
  194.0 3.5 %all-to-all-start.1 = ((f32[32,1,128]{2,1,0:T(1,128)}), f32[32,1,128]{2,1,0:T(1,128)S(1)}, u32[]{:S(2)}, u32[]{:S(2)}) async-start(f32[32,1,128]{2,1,0:T(1,128)} %broadcast_in_dim.34), calls=%async_computation.1 | async-start | bytes 32768 | tf_op jit(solution)/shard_map/all_to_all | solution.py:1075
  198.3 6.3 %all-to-all-done.1 = f32[32,1,128]{2,1,0:T(1,128)S(1)} async-done(((f32[32,1,128]{2,1,0:T(1,128)}), f32[32,1,128]{2,1,0:T(1,128)S(1)}, u32[]{:S(2)}, u32[]{:S(2)}) %all-to-all-start.1) | async-done | bytes 16416 | tf_op jit(solution)/shard_map/all_to_all | solution.py:1075
  (178 shorter events, 29.6 us)
Async XLA Ops:
  3.2 23.5 %collective-permute-start = (bf16[1,296,128]{2,1,0:T(8,128)(2,1)S(1)}, bf16[1,296,128]{2,1,0:T(8,128)(2,1)S(1)}, u32[]{:S(2)}, u32[]{:S(2)}) collective-permute-start(bf16[1,296,128]{2,1,0:T(8,128)(2,1)S(1)} %maximum_bitcast_fusion), channel_id=1, source_target_pairs={{0,8},{1,9},{2,10},{3,11},{4,12},{5,13},{6,14},{7,15},{8,0},{9,1},... | collective-permute-start | bytes 227336 | tf_op jit(solution)/shard_map/ppermute | solution.py:966
  6.3 20.4 %collective-permute-start.1 = (bf16[1,296,128]{2,1,0:T(8,128)(2,1)S(1)}, bf16[1,296,128]{2,1,0:T(8,128)(2,1)S(1)}, u32[]{:S(2)}, u32[]{:S(2)}) collective-permute-start(bf16[1,296,128]{2,1,0:T(8,128)(2,1)S(1)} %maximum_bitcast_fusion), channel_id=1, source_target_pairs={{0,16},{1,17},{2,18},{3,19},{4,20},{5,21},{6,22},{7,23},{8,24},{9,... | collective-permute-start | bytes 227336 | tf_op jit(solution)/shard_map/ppermute | solution.py:966
  9.6 9.8 %collective-permute-start.6 = (bf16[1,280,128]{2,1,0:T(8,128)(2,1)S(1)}, bf16[1,280,128]{2,1,0:T(8,128)(2,1)S(1)}, u32[]{:S(2)}, u32[]{:S(2)}) collective-permute-start(bf16[1,280,128]{2,1,0:T(8,128)(2,1)S(1)} %maximum_bitcast_fusion.1), channel_id=1, source_target_pairs={{0,8},{1,9},{2,10},{3,11},{4,12},{5,13},{6,14},{7,15},{8,0},{9,1},... | collective-permute-start | bytes 215048 | tf_op jit(solution)/shard_map/ppermute | solution.py:966
  10.2 12.9 %collective-permute-start.7 = (bf16[1,280,128]{2,1,0:T(8,128)(2,1)S(1)}, bf16[1,280,128]{2,1,0:T(8,128)(2,1)S(1)}, u32[]{:S(2)}, u32[]{:S(2)}) collective-permute-start(bf16[1,280,128]{2,1,0:T(8,128)(2,1)S(1)} %maximum_bitcast_fusion.1), channel_id=1, source_target_pairs={{0,16},{1,17},{2,18},{3,19},{4,20},{5,21},{6,22},{7,23},{8,24},{9,... | collective-permute-start | bytes 215048 | tf_op jit(solution)/shard_map/ppermute | solution.py:966
  10.2 12.9 %collective-permute-start.8 = (bf16[1,280,128]{2,1,0:T(8,128)(2,1)S(1)}, bf16[1,280,128]{2,1,0:T(8,128)(2,1)S(1)}, u32[]{:S(2)}, u32[]{:S(2)}) collective-permute-start(bf16[1,280,128]{2,1,0:T(8,128)(2,1)S(1)} %maximum_bitcast_fusion.1), channel_id=1, source_target_pairs={{0,24},{1,25},{2,26},{3,27},{4,28},{5,29},{6,30},{7,31},{8,16},{9,... | collective-permute-start | bytes 215048 | tf_op jit(solution)/shard_map/ppermute | solution.py:966
  15.4 24.3 %all-to-all-start = ((f32[32,1,128]{2,1,0:T(1,128)}), f32[32,1,128]{2,1,0:T(1,128)S(1)}, u32[]{:S(2)}, u32[]{:S(2)}) async-start(f32[32,1,128]{2,1,0:T(1,128)} %broadcast_in_dim.14), calls=%async_computation | async-start | bytes 32768 | tf_op jit(solution)/shard_map/all_to_all | solution.py:1075
  19.5 7.2 %collective-permute-start.2 = (bf16[1,296,128]{2,1,0:T(8,128)(2,1)S(1)}, bf16[1,296,128]{2,1,0:T(8,128)(2,1)S(1)}, u32[]{:S(2)}, u32[]{:S(2)}) collective-permute-start(bf16[1,296,128]{2,1,0:T(8,128)(2,1)S(1)} %maximum_bitcast_fusion), channel_id=1, source_target_pairs={{0,24},{1,25},{2,26},{3,27},{4,28},{5,29},{6,30},{7,31},{8,16},{9,... | collective-permute-start | bytes 227336 | tf_op jit(solution)/shard_map/ppermute | solution.py:966
  23.1 8.7 %collective-permute-start.9 = (bf16[4,280,128]{2,1,0:T(8,128)(2,1)S(1)}, bf16[4,280,128]{2,1,0:T(8,128)(2,1)S(1)}, u32[]{:S(2)}, u32[]{:S(2)}) collective-permute-start(bf16[4,280,128]{2,1,0:T(8,128)(2,1)S(1)} %pad_maximum_fusion.1), channel_id=1, source_target_pairs={{0,4},{1,5},{2,6},{3,7},{4,0},{5,1},{6,2},{7,3},{8,12},{9,13},{10,... | collective-permute-start | bytes 860168 | tf_op jit(solution)/shard_map/ppermute | solution.py:966
  26.7 9.7 %collective-permute-start.3 = (bf16[4,296,128]{2,1,0:T(8,128)(2,1)S(1)}, bf16[4,296,128]{2,1,0:T(8,128)(2,1)S(1)}, u32[]{:S(2)}, u32[]{:S(2)}) collective-permute-start(bf16[4,296,128]{2,1,0:T(8,128)(2,1)S(1)} %pad_maximum_fusion), channel_id=1, source_target_pairs={{0,2},{1,3},{2,0},{3,1},{4,6},{5,7},{6,4},{7,5},{8,10},{9,11},{10,... | collective-permute-start | bytes 909320 | tf_op jit(solution)/shard_map/ppermute | solution.py:966
  32.6 15.2 %collective-permute-start.10 = (bf16[8,280,128]{2,1,0:T(8,128)(2,1)}, bf16[8,280,128]{2,1,0:T(8,128)(2,1)}, u32[]{:S(2)}, u32[]{:S(2)}) collective-permute-start(bf16[8,280,128]{2,1,0:T(8,128)(2,1)} %get-tuple-element.128), channel_id=1, source_target_pairs={{0,2},{1,3},{2,0},{3,1},{4,6},{5,7},{6,4},{7,5},{8,10},{9,11},{10,... | collective-permute-start | bytes 1720328 | tf_op jit(solution)/shard_map/ppermute | solution.py:966
  37.2 13.6 %collective-permute-start.4 = (bf16[8,296,128]{2,1,0:T(8,128)(2,1)}, bf16[8,296,128]{2,1,0:T(8,128)(2,1)}, u32[]{:S(2)}, u32[]{:S(2)}) collective-permute-start(bf16[8,296,128]{2,1,0:T(8,128)(2,1)} %get-tuple-element.126), channel_id=1, source_target_pairs={{0,4},{1,5},{2,6},{3,7},{4,0},{5,1},{6,2},{7,3},{8,12},{9,13},{10,... | collective-permute-start | bytes 1818632 | tf_op jit(solution)/shard_map/ppermute | solution.py:966
  49.8 5.0 %collective-permute-start.11 = (bf16[16,280,128]{2,1,0:T(8,128)(2,1)}, bf16[16,280,128]{2,1,0:T(8,128)(2,1)}, u32[]{:S(2)}, u32[]{:S(2)}) collective-permute-start(bf16[16,280,128]{2,1,0:T(8,128)(2,1)} %constant_dynamic-update-slice_fusion.16.refs_1_), channel_id=1, source_target_pairs={{0,1},{1,0},{2,3},{3,2},{4,5},{5,4},{6,7},{7,6},{8,9},{9,8},{10,11... | collective-permute-start | bytes 3440648 | tf_op jit(solution)/shard_map/ppermute | solution.py:966
  52.0 8.1 %collective-permute-start.5 = (bf16[16,296,128]{2,1,0:T(8,128)(2,1)S(1)}, bf16[16,296,128]{2,1,0:T(8,128)(2,1)S(1)}, u32[]{:S(2)}, u32[]{:S(2)}) collective-permute-start(bf16[16,296,128]{2,1,0:T(8,128)(2,1)S(1)} %constant_dynamic-update-slice_fusion.5.refs_3_.refs_1_), channel_id=1, source_target_pairs={{0,1},{1,0},{2,3},{3,2},{4,5},{5,4},{6,7},{7,6},{8,9},{9,8},{10,11... | collective-permute-start | bytes 3637256 | tf_op jit(solution)/shard_map/ppermute | solution.py:966
  106.2 22.7 %collective-permute-start.30 = (bf16[16,72,128]{2,1,0:T(8,128)(2,1)S(1)}, bf16[16,72,128]{2,1,0:T(8,128)(2,1)S(1)}, u32[]{:S(2)}, u32[]{:S(2)}) collective-permute-start(bf16[16,72,128]{2,1,0:T(8,128)(2,1)S(1)} %get-tuple-element.89), channel_id=1, source_target_pairs={{0,1},{1,0},{2,3},{3,2},{4,5},{5,4},{6,7},{7,6},{8,9},{9,8},{10,11... | collective-permute-start | bytes 884744 | tf_op jit(solution)/shard_map/ppermute | solution.py:966
  106.7 22.7 %collective-permute-start.36 = (bf16[16,80,128]{2,1,0:T(8,128)(2,1)S(1)}, bf16[16,80,128]{2,1,0:T(8,128)(2,1)S(1)}, u32[]{:S(2)}, u32[]{:S(2)}) collective-permute-start(bf16[16,80,128]{2,1,0:T(8,128)(2,1)S(1)} %get-tuple-element.91), channel_id=1, source_target_pairs={{0,1},{1,0},{2,3},{3,2},{4,5},{5,4},{6,7},{7,6},{8,9},{9,8},{10,11... | collective-permute-start | bytes 983048 | tf_op jit(solution)/shard_map/ppermute | solution.py:966
  122.5 40.0 %collective-permute-start.18 = (bf16[16,176,128]{2,1,0:T(8,128)(2,1)}, bf16[16,176,128]{2,1,0:T(8,128)(2,1)S(1)}, u32[]{:S(2)}, u32[]{:S(2)}) collective-permute-start(bf16[16,176,128]{2,1,0:T(8,128)(2,1)} %get-tuple-element.85), channel_id=1, source_target_pairs={{0,1},{1,0},{2,3},{3,2},{4,5},{5,4},{6,7},{7,6},{8,9},{9,8},{10,11... | collective-permute-start | bytes 2162696 | tf_op jit(solution)/shard_map/ppermute | solution.py:966
  122.9 37.7 %collective-permute-start.24 = (bf16[16,168,128]{2,1,0:T(8,128)(2,1)}, bf16[16,168,128]{2,1,0:T(8,128)(2,1)S(1)}, u32[]{:S(2)}, u32[]{:S(2)}) collective-permute-start(bf16[16,168,128]{2,1,0:T(8,128)(2,1)} %get-tuple-element.87), channel_id=1, source_target_pairs={{0,1},{1,0},{2,3},{3,2},{4,5},{5,4},{6,7},{7,6},{8,9},{9,8},{10,11... | collective-permute-start | bytes 2064392 | tf_op jit(solution)/shard_map/ppermute | solution.py:966
  128.4 2.6 %collective-permute-start.12 = (bf16[16,80,128]{2,1,0:T(8,128)(2,1)S(1)}, bf16[16,80,128]{2,1,0:T(8,128)(2,1)S(1)}, u32[]{:S(2)}, u32[]{:S(2)}) collective-permute-start(bf16[16,80,128]{2,1,0:T(8,128)(2,1)S(1)} %get-tuple-element.83), channel_id=1, source_target_pairs={{0,1},{1,0},{2,3},{3,2},{4,5},{5,4},{6,7},{7,6},{8,9},{9,8},{10,11... | collective-permute-start | bytes 983048 | tf_op jit(solution)/shard_map/ppermute | solution.py:966
  129.0 5.8 %collective-permute-start.31 = (bf16[8,72,128]{2,1,0:T(8,128)(2,1)S(1)}, bf16[8,72,128]{2,1,0:T(8,128)(2,1)S(1)}, u32[]{:S(2)}, u32[]{:S(2)}) collective-permute-start(bf16[8,72,128]{2,1,0:T(8,128)(2,1)S(1)} %slice.328), channel_id=1, source_target_pairs={{0,4},{1,5},{2,6},{3,7},{4,0},{5,1},{6,2},{7,3},{8,12},{9,13},{10,... | collective-permute-start | bytes 442376 | tf_op jit(solution)/shard_map/ppermute | solution.py:966
  129.5 7.2 %collective-permute-start.37 = (bf16[8,80,128]{2,1,0:T(8,128)(2,1)S(1)}, bf16[8,80,128]{2,1,0:T(8,128)(2,1)S(1)}, u32[]{:S(2)}, u32[]{:S(2)}) collective-permute-start(bf16[8,80,128]{2,1,0:T(8,128)(2,1)S(1)} %slice.326), channel_id=1, source_target_pairs={{0,2},{1,3},{2,0},{3,1},{4,6},{5,7},{6,4},{7,5},{8,10},{9,11},{10,... | collective-permute-start | bytes 491528 | tf_op jit(solution)/shard_map/ppermute | solution.py:966
  131.1 12.7 %collective-permute-start.13 = (bf16[8,80,128]{2,1,0:T(8,128)(2,1)S(1)}, bf16[8,80,128]{2,1,0:T(8,128)(2,1)S(1)}, u32[]{:S(2)}, u32[]{:S(2)}) collective-permute-start(bf16[8,80,128]{2,1,0:T(8,128)(2,1)S(1)} %slice.327), channel_id=1, source_target_pairs={{0,2},{1,3},{2,0},{3,1},{4,6},{5,7},{6,4},{7,5},{8,10},{9,11},{10,... | collective-permute-start | bytes 491528 | tf_op jit(solution)/shard_map/ppermute | solution.py:966
  134.9 5.6 %collective-permute-start.32 = (bf16[4,72,128]{2,1,0:T(8,128)(2,1)S(1)}, bf16[4,72,128]{2,1,0:T(8,128)(2,1)S(1)}, u32[]{:S(2)}, u32[]{:S(2)}) collective-permute-start(bf16[4,72,128]{2,1,0:T(8,128)(2,1)S(1)} %slice.331), channel_id=1, source_target_pairs={{0,2},{1,3},{2,0},{3,1},{4,6},{5,7},{6,4},{7,5},{8,10},{9,11},{10,... | collective-permute-start | bytes 221192 | tf_op jit(solution)/shard_map/ppermute | solution.py:966
  140.5 4.5 %collective-permute-start.33 = (bf16[1,72,128]{2,1,0:T(8,128)(2,1)S(1)}, bf16[1,72,128]{2,1,0:T(8,128)(2,1)S(1)}, u32[]{:S(2)}, u32[]{:S(2)}) collective-permute-start(bf16[1,72,128]{2,1,0:T(8,128)(2,1)S(1)} %get-tuple-element.150), channel_id=1, source_target_pairs={{0,8},{1,9},{2,10},{3,11},{4,12},{5,13},{6,14},{7,15},{8,0},{9,1},... | collective-permute-start | bytes 55304 | tf_op jit(solution)/shard_map/ppermute | solution.py:966
  140.8 6.0 %collective-permute-start.34 = (bf16[1,72,128]{2,1,0:T(8,128)(2,1)S(1)}, bf16[1,72,128]{2,1,0:T(8,128)(2,1)S(1)}, u32[]{:S(2)}, u32[]{:S(2)}) collective-permute-start(bf16[1,72,128]{2,1,0:T(8,128)(2,1)S(1)} %get-tuple-element.152), channel_id=1, source_target_pairs={{0,16},{1,17},{2,18},{3,19},{4,20},{5,21},{6,22},{7,23},{8,24},{9,... | collective-permute-start | bytes 55304 | tf_op jit(solution)/shard_map/ppermute | solution.py:966
  143.8 5.6 %collective-permute-start.35 = (bf16[1,72,128]{2,1,0:T(8,128)(2,1)S(1)}, bf16[1,72,128]{2,1,0:T(8,128)(2,1)S(1)}, u32[]{:S(2)}, u32[]{:S(2)}) collective-permute-start(bf16[1,72,128]{2,1,0:T(8,128)(2,1)S(1)} %get-tuple-element.151), channel_id=1, source_target_pairs={{0,24},{1,25},{2,26},{3,27},{4,28},{5,29},{6,30},{7,31},{8,16},{9,... | collective-permute-start | bytes 55304 | tf_op jit(solution)/shard_map/ppermute | solution.py:966
  145.1 4.9 %collective-permute-start.38 = (bf16[4,80,128]{2,1,0:T(8,128)(2,1)S(1)}, bf16[4,80,128]{2,1,0:T(8,128)(2,1)S(1)}, u32[]{:S(2)}, u32[]{:S(2)}) collective-permute-start(bf16[4,80,128]{2,1,0:T(8,128)(2,1)S(1)} %slice.329), channel_id=1, source_target_pairs={{0,4},{1,5},{2,6},{3,7},{4,0},{5,1},{6,2},{7,3},{8,12},{9,13},{10,... | collective-permute-start | bytes 245768 | tf_op jit(solution)/shard_map/ppermute | solution.py:966
  146.9 6.0 %collective-permute-start.14 = (bf16[4,80,128]{2,1,0:T(8,128)(2,1)S(1)}, bf16[4,80,128]{2,1,0:T(8,128)(2,1)S(1)}, u32[]{:S(2)}, u32[]{:S(2)}) collective-permute-start(bf16[4,80,128]{2,1,0:T(8,128)(2,1)S(1)} %slice.330), channel_id=1, source_target_pairs={{0,4},{1,5},{2,6},{3,7},{4,0},{5,1},{6,2},{7,3},{8,12},{9,13},{10,... | collective-permute-start | bytes 245768 | tf_op jit(solution)/shard_map/ppermute | solution.py:966
  150.0 4.5 %collective-permute-start.39 = (bf16[1,80,128]{2,1,0:T(8,128)(2,1)S(1)}, bf16[1,80,128]{2,1,0:T(8,128)(2,1)S(1)}, u32[]{:S(2)}, u32[]{:S(2)}) collective-permute-start(bf16[1,80,128]{2,1,0:T(8,128)(2,1)S(1)} %get-tuple-element.136), channel_id=1, source_target_pairs={{0,8},{1,9},{2,10},{3,11},{4,12},{5,13},{6,14},{7,15},{8,0},{9,1},... | collective-permute-start | bytes 61448 | tf_op jit(solution)/shard_map/ppermute | solution.py:966
  150.1 4.9 %collective-permute-start.40 = (bf16[1,80,128]{2,1,0:T(8,128)(2,1)S(1)}, bf16[1,80,128]{2,1,0:T(8,128)(2,1)S(1)}, u32[]{:S(2)}, u32[]{:S(2)}) collective-permute-start(bf16[1,80,128]{2,1,0:T(8,128)(2,1)S(1)} %get-tuple-element.138), channel_id=1, source_target_pairs={{0,16},{1,17},{2,18},{3,19},{4,20},{5,21},{6,22},{7,23},{8,24},{9,... | collective-permute-start | bytes 61448 | tf_op jit(solution)/shard_map/ppermute | solution.py:966
  152.9 5.8 %collective-permute-start.41 = (bf16[1,80,128]{2,1,0:T(8,128)(2,1)S(1)}, bf16[1,80,128]{2,1,0:T(8,128)(2,1)S(1)}, u32[]{:S(2)}, u32[]{:S(2)}) collective-permute-start(bf16[1,80,128]{2,1,0:T(8,128)(2,1)S(1)} %get-tuple-element.137), channel_id=1, source_target_pairs={{0,24},{1,25},{2,26},{3,27},{4,28},{5,29},{6,30},{7,31},{8,16},{9,... | collective-permute-start | bytes 61448 | tf_op jit(solution)/shard_map/ppermute | solution.py:966
  154.5 9.8 %collective-permute-start.15 = (bf16[1,80,128]{2,1,0:T(8,128)(2,1)S(1)}, bf16[1,80,128]{2,1,0:T(8,128)(2,1)S(1)}, u32[]{:S(2)}, u32[]{:S(2)}) collective-permute-start(bf16[1,80,128]{2,1,0:T(8,128)(2,1)S(1)} %get-tuple-element.139), channel_id=1, source_target_pairs={{0,8},{1,9},{2,10},{3,11},{4,12},{5,13},{6,14},{7,15},{8,0},{9,1},... | collective-permute-start | bytes 61448 | tf_op jit(solution)/shard_map/ppermute | solution.py:966
  155.0 9.3 %collective-permute-start.16 = (bf16[1,80,128]{2,1,0:T(8,128)(2,1)S(1)}, bf16[1,80,128]{2,1,0:T(8,128)(2,1)S(1)}, u32[]{:S(2)}, u32[]{:S(2)}) collective-permute-start(bf16[1,80,128]{2,1,0:T(8,128)(2,1)S(1)} %get-tuple-element.141), channel_id=1, source_target_pairs={{0,16},{1,17},{2,18},{3,19},{4,20},{5,21},{6,22},{7,23},{8,24},{9,... | collective-permute-start | bytes 61448 | tf_op jit(solution)/shard_map/ppermute | solution.py:966
  158.7 5.6 %collective-permute-start.17 = (bf16[1,80,128]{2,1,0:T(8,128)(2,1)S(1)}, bf16[1,80,128]{2,1,0:T(8,128)(2,1)S(1)}, u32[]{:S(2)}, u32[]{:S(2)}) collective-permute-start(bf16[1,80,128]{2,1,0:T(8,128)(2,1)S(1)} %get-tuple-element.140), channel_id=1, source_target_pairs={{0,24},{1,25},{2,26},{3,27},{4,28},{5,29},{6,30},{7,31},{8,16},{9,... | collective-permute-start | bytes 61448 | tf_op jit(solution)/shard_map/ppermute | solution.py:966
  161.0 8.6 %collective-permute-start.25 = (bf16[8,168,128]{2,1,0:T(8,128)(2,1)S(1)}, bf16[8,168,128]{2,1,0:T(8,128)(2,1)S(1)}, u32[]{:S(2)}, u32[]{:S(2)}) collective-permute-start(bf16[8,168,128]{2,1,0:T(8,128)(2,1)S(1)} %slice.323), channel_id=1, source_target_pairs={{0,4},{1,5},{2,6},{3,7},{4,0},{5,1},{6,2},{7,3},{8,12},{9,13},{10,... | collective-permute-start | bytes 1032200 | tf_op jit(solution)/shard_map/ppermute | solution.py:966
  162.8 8.4 %collective-permute-start.19 = (bf16[8,176,128]{2,1,0:T(8,128)(2,1)S(1)}, bf16[8,176,128]{2,1,0:T(8,128)(2,1)S(1)}, u32[]{:S(2)}, u32[]{:S(2)}) collective-permute-start(bf16[8,176,128]{2,1,0:T(8,128)(2,1)S(1)} %slice.322), channel_id=1, source_target_pairs={{0,2},{1,3},{2,0},{3,1},{4,6},{5,7},{6,4},{7,5},{8,10},{9,11},{10,... | collective-permute-start | bytes 1081352 | tf_op jit(solution)/shard_map/ppermute | solution.py:966
  169.7 5.5 %collective-permute-start.26 = (bf16[4,168,128]{2,1,0:T(8,128)(2,1)S(1)}, bf16[4,168,128]{2,1,0:T(8,128)(2,1)S(1)}, u32[]{:S(2)}, u32[]{:S(2)}) collective-permute-start(bf16[4,168,128]{2,1,0:T(8,128)(2,1)S(1)} %slice.325), channel_id=1, source_target_pairs={{0,2},{1,3},{2,0},{3,1},{4,6},{5,7},{6,4},{7,5},{8,10},{9,11},{10,... | collective-permute-start | bytes 516104 | tf_op jit(solution)/shard_map/ppermute | solution.py:966
  171.3 8.4 %collective-permute-start.20 = (bf16[4,176,128]{2,1,0:T(8,128)(2,1)S(1)}, bf16[4,176,128]{2,1,0:T(8,128)(2,1)S(1)}, u32[]{:S(2)}, u32[]{:S(2)}) collective-permute-start(bf16[4,176,128]{2,1,0:T(8,128)(2,1)S(1)} %slice.324), channel_id=1, source_target_pairs={{0,4},{1,5},{2,6},{3,7},{4,0},{5,1},{6,2},{7,3},{8,12},{9,13},{10,... | collective-permute-start | bytes 540680 | tf_op jit(solution)/shard_map/ppermute | solution.py:966
  175.2 30.8 %copy-start.5 = (f32[44032]{0:T(1024)S(1)}, f32[44032]{0:T(1024)}, u32[]{:S(2)}) copy-start(f32[44032]{0:T(1024)} %param.29) | copy-start | bytes 528388
  175.2 30.8 %copy-start.8 = (f32[44032]{0:T(1024)S(1)}, f32[44032]{0:T(1024)}, u32[]{:S(2)}) copy-start(f32[44032]{0:T(1024)} %param.31) | copy-start | bytes 528388
  175.2 30.8 %copy-start.9 = (f32[44032]{0:T(1024)S(1)}, f32[44032]{0:T(1024)}, u32[]{:S(2)}) copy-start(f32[44032]{0:T(1024)} %param.30) | copy-start | bytes 528388
  175.2 8.3 %collective-permute-start.27 = (bf16[1,168,128]{2,1,0:T(8,128)(2,1)S(1)}, bf16[1,168,128]{2,1,0:T(8,128)(2,1)S(1)}, u32[]{:S(2)}, u32[]{:S(2)}) collective-permute-start(bf16[1,168,128]{2,1,0:T(8,128)(2,1)S(1)} %get-tuple-element.133), channel_id=1, source_target_pairs={{0,8},{1,9},{2,10},{3,11},{4,12},{5,13},{6,14},{7,15},{8,0},{9,1},... | collective-permute-start | bytes 129032 | tf_op jit(solution)/shard_map/ppermute | solution.py:966
  175.3 9.0 %collective-permute-start.28 = (bf16[1,168,128]{2,1,0:T(8,128)(2,1)S(1)}, bf16[1,168,128]{2,1,0:T(8,128)(2,1)S(1)}, u32[]{:S(2)}, u32[]{:S(2)}) collective-permute-start(bf16[1,168,128]{2,1,0:T(8,128)(2,1)S(1)} %get-tuple-element.135), channel_id=1, source_target_pairs={{0,16},{1,17},{2,18},{3,19},{4,20},{5,21},{6,22},{7,23},{8,24},{9,... | collective-permute-start | bytes 129032 | tf_op jit(solution)/shard_map/ppermute | solution.py:966
  179.0 5.8 %collective-permute-start.29 = (bf16[1,168,128]{2,1,0:T(8,128)(2,1)S(1)}, bf16[1,168,128]{2,1,0:T(8,128)(2,1)S(1)}, u32[]{:S(2)}, u32[]{:S(2)}) collective-permute-start(bf16[1,168,128]{2,1,0:T(8,128)(2,1)S(1)} %get-tuple-element.134), channel_id=1, source_target_pairs={{0,24},{1,25},{2,26},{3,27},{4,28},{5,29},{6,30},{7,31},{8,16},{9,... | collective-permute-start | bytes 129032 | tf_op jit(solution)/shard_map/ppermute | solution.py:966
  179.7 27.2 %copy-start.12 = (f32[9216]{0:T(1024)S(1)}, f32[9216]{0:T(1024)}, u32[]{:S(2)}) copy-start(f32[9216]{0:T(1024)} %param.32) | copy-start | bytes 110596
  179.8 5.1 %collective-permute-start.21 = (bf16[1,176,128]{2,1,0:T(8,128)(2,1)S(1)}, bf16[1,176,128]{2,1,0:T(8,128)(2,1)S(1)}, u32[]{:S(2)}, u32[]{:S(2)}) collective-permute-start(bf16[1,176,128]{2,1,0:T(8,128)(2,1)S(1)} %get-tuple-element.130), channel_id=1, source_target_pairs={{0,8},{1,9},{2,10},{3,11},{4,12},{5,13},{6,14},{7,15},{8,0},{9,1},... | collective-permute-start | bytes 135176 | tf_op jit(solution)/shard_map/ppermute | solution.py:966
  179.9 5.7 %collective-permute-start.22 = (bf16[1,176,128]{2,1,0:T(8,128)(2,1)S(1)}, bf16[1,176,128]{2,1,0:T(8,128)(2,1)S(1)}, u32[]{:S(2)}, u32[]{:S(2)}) collective-permute-start(bf16[1,176,128]{2,1,0:T(8,128)(2,1)S(1)} %get-tuple-element.132), channel_id=1, source_target_pairs={{0,16},{1,17},{2,18},{3,19},{4,20},{5,21},{6,22},{7,23},{8,24},{9,... | collective-permute-start | bytes 135176 | tf_op jit(solution)/shard_map/ppermute | solution.py:966
  183.6 5.8 %collective-permute-start.23 = (bf16[1,176,128]{2,1,0:T(8,128)(2,1)S(1)}, bf16[1,176,128]{2,1,0:T(8,128)(2,1)S(1)}, u32[]{:S(2)}, u32[]{:S(2)}) collective-permute-start(bf16[1,176,128]{2,1,0:T(8,128)(2,1)S(1)} %get-tuple-element.131), channel_id=1, source_target_pairs={{0,24},{1,25},{2,26},{3,27},{4,28},{5,29},{6,30},{7,31},{8,16},{9,... | collective-permute-start | bytes 135176 | tf_op jit(solution)/shard_map/ppermute | solution.py:966
  194.0 10.6 %all-to-all-start.1 = ((f32[32,1,128]{2,1,0:T(1,128)}), f32[32,1,128]{2,1,0:T(1,128)S(1)}, u32[]{:S(2)}, u32[]{:S(2)}) async-start(f32[32,1,128]{2,1,0:T(1,128)} %broadcast_in_dim.34), calls=%async_computation.1 | async-start | bytes 32768 | tf_op jit(solution)/shard_map/all_to_all | solution.py:1075
  (19 other events, 250.6 us)
where the time goes:
time: 210 us; the launch traced here: 209 us
  Pallas kernels  70.5 us (34%)
  starting transfers between devices  61.4 us (29%)
  waiting for transfers between devices  41.2 us (20%)
  local copies, waits for them, and re-layouts  17.5 us (8%)
  other arithmetic  11.8 us (6%)
  between operations  7.17 us (3%)
    pallas_call x7, Pallas kernels, run(): pl.pallas_call(kernel, out_shape=out_leaves, in_specs=[pl.BlockSpec(memor...  70.5 us
    ppermute x42, starting transfers between devices, swap(): lax.ppermute(values, AXES, [(here, here ^ mask) for here in range(count)])  55 us
    ppermute x42, waiting for transfers between devices, swap(): lax.ppermute(values, AXES, [(here, here ^ mask) for here in range(count)])  34.8 us
    unnamed x55, local copies, waits for them, and re-layouts  6.64 us
    all_to_all x2, waiting for transfers between devices, scalar_sums(): arrived = lax.all_to_all(sent, AXES, 0, 0, tiled=True)  6.34 us
    all_to_all x2, starting transfers between devices, scalar_sums(): arrived = lax.all_to_all(sent, AXES, 0, 0, tiled=True)  6.33 us
    concatenate x4, local copies, waits for them, and re-layouts, gather(): held = jnp.concatenate([held] + arrived, axis=0)  4.66 us
  transfers between devices with their start and end apart: 44, of which 16 were waited for; matrix products, arithmetic and copies ran while one was open for 9% of the time, Pallas kernels for 12%

commit v1 on v0

--- a/solution.py
+++ b/solution.py
@@ -88,7 +88,7 @@
         body(pl.multiple_of(number * size, size))
         return carry
 
-    lax.fori_loop(0, total // size, step, 0)
+    lax.fori_loop(0, total // size, step, 0, unroll=True)
 
 
 def widen(pieces, places, me, stage):
@@ -149,7 +149,7 @@
             return carry
 
         first = load(0, image, image * LOW)
-        carry = lax.fori_loop(0, 4, step, tuple(jnp.zeros((8, width), f32) for _ in first))
+        carry = lax.fori_loop(0, 4, step, tuple(jnp.zeros((8, width), f32) for _ in first), unroll=True)
         sums.append([jnp.sum(c, axis=0, keepdims=True) for c in carry])
     return [jnp.concatenate(list(group), axis=0) for group in zip(*sums)]
 
@@ -192,7 +192,7 @@
                 body(phase, image, inside, image * LOW + inside)
             return carry
 
-        lax.fori_loop(0, LOW // size, step, 0)
+        lax.fori_loop(0, LOW // size, step, 0, unroll=True)
 
 
 def clear_edges(wide):
@@ -224,16 +224,11 @@
 
 
 def conv_low_back(wide, kern):
-    width = wide.shape[2] // 3
     total = None
     for row_tap in range(3):
-        for col_tap in range(3):
-            tap = row_tap * 3 + col_tap
-            part = mm_nt(
-                wide_rows(wide, 1 - row_tap, (2 - col_tap) * width, (3 - col_tap) * width),
-                kern[tap * C2 : (tap + 1) * C2, :],
-            )
-            total = part if total is None else total + part
+        taps = [kern[(row_tap * 3 + col_tap) * C2 : (row_tap * 3 + col_tap + 1) * C2, :] for col_tap in (2, 1, 0)]
+        part = mm_nt(wide_rows(wide, 1 - row_tap, 0, 3 * C2), jnp.concatenate(taps, axis=1))
+        total = part if total is None else total + part
     return total
 
 
@@ -771,13 +766,10 @@
     total = None
     for row_phase in range(2):
         for slot in range(2):
-            row_off = row_phase - 1 + slot
-            for col_off in range(3):
-                part = mm_nt(
-                    wide_rows(wides[row_phase], -row_off, (2 - col_off) * C2, (3 - col_off) * C2),
-                    kern_up[row_phase, (slot * 3 + col_off) * C2 : (slot * 3 + col_off + 1) * C2, :],
-                )
-                total = part if total is None else total + part
+            base = slot * 3 * C2
+            taps = [kern_up[row_phase, base + at * C2 : base + (at + 1) * C2, :] for at in (2, 1, 0)]
+            part = mm_nt(wide_rows(wides[row_phase], 1 - row_phase - slot, 0, 3 * C2), jnp.concatenate(taps, axis=1))
+            total = part if total is None else total + part
     grad_attn[...] = total
     width = 3 * C1
 
@@ -823,7 +815,7 @@
         in_specs=[pl.BlockSpec(memory_space=pltpu.SMEM)] + [whole] * (len(in_leaves) - 1),
         out_specs=[whole] * len(out_leaves),
         scratch_shapes=scratch,
-        compiler_params=pltpu.CompilerParams(vmem_limit_bytes=52 * 2**20),
+        compiler_params=pltpu.CompilerParams(vmem_limit_bytes=62 * 2**20),
     )(*in_leaves)
     return jax.tree.unflatten(out_tree, results)
 
@@ -832,97 +824,85 @@
     return pltpu.VMEM((IMGS, PADDED, width), dtype)
 
 
-def forward_stem(me, weights, noisy):
-    arrays, places = weights
+SAVED = dict(
+    stage=((RES_ROWS, LANES), f32), block_out=((HEAD_ROWS, LANES), f32),
+    taps=((72, 4 * ROWS), f32), low_taps=((72, 4 * ROWS), f32), narrow=((72, LANES), f32),
+    top=((4, ROWS, C1), f32), down=((ROWS, C2), f32), inner=((ROWS, C2), f32), res_out=((ROWS, C2), f32),
+    act_one=((ROWS, C2), bf16), act_two=((ROWS, C2), bf16), attn_low=((ROWS, C2), bf16), normed=((ROWS, C2), bf16),
+    qkv=((ROWS, 3 * C2), bf16), probs=((IMGS, LOW, LOW), f32), mixed=((ROWS, C2), bf16),
+    merged=((4, ROWS, C1), f32), act=((4, ROWS, C1), bf16), skip=((4, ROWS, C1), f32),
+    grad_attn=((ROWS, C2), f32), grad_res=((ROWS, C2), f32), grad_act=((ROWS, C2), f32),
+    grad_low=((ROWS, C2), bf16), grad_mixed=((ROWS, C2), bf16), grad_qkv=((ROWS, 3 * C2), bf16),
+    dense_one=((TDIM, TEMB), bf16), dense_two=((TEMB, C2), bf16), kern_down=((9 * C1, C2), bf16),
+    kern_first=((9 * C2, C2), bf16), kern_second=((9 * C2, C2), bf16), kern_qkv=((C2, 3 * C2), bf16),
+    kern_proj=((C2, C2), bf16), kern_up=((2, 6 * C2, C2), bf16),
+    hidden_pre=((8, TEMB), f32), res_stats=((16, C2), f32), res_gains=((8, C2), f32),
+    attn_stats=((8, C2), f32), attn_gains=((8, C2), f32),
+    wide=((IMGS, PADDED, 3 * C2), bf16), wide_zero=((IMGS, PADDED, 3 * C2), bf16),
+    wide_one=((IMGS, PADDED, 3 * C2), bf16), boxes=((IMGS, PADDED, 6 * C1), f32),
+)
+
+
+class Named:
+    def __init__(self, names, refs):
+        self.__dict__.update(zip(names, refs))
+
+
+def whole_step(places, leaving, me, gathered, noisy, clean, factor, embed, loss, sent, *refs):
+    own = Named(SAVED, refs)
+    stem_wide, stem_wide_zero = own.wide.at[:, :, 0 : 3 * C1], own.wide_zero.at[:, :, 0 : 3 * C1]
+    stem_forward(
+        places[0], me, gathered[0], noisy, own.top, own.down, own.kern_down, own.stage, own.taps, stem_wide, stem_wide_zero
+    )
+    res_forward(
+        places[1], me, gathered[1], own.down, embed,
+        own.inner, own.res_out, own.act_one, own.act_two, own.kern_first, own.kern_second, own.dense_two,
+        own.hidden_pre, own.res_stats, own.res_gains,
+        own.stage, own.dense_one, own.wide,
+    )
+    attn_forward(
+        places[2], me, gathered[2], own.res_out,
+        own.attn_low, own.normed, own.qkv, own.probs, own.mixed, own.kern_qkv, own.kern_proj,
+        own.attn_stats, own.attn_gains,
+        own.stage,
+    )
+    head_step(
+        places[3], leaving[3], me, gathered[3], own.attn_low, own.top, clean, factor,
+        own.grad_attn, own.skip, loss, sent[3], own.block_out,
+        own.stage, own.wide, own.kern_up, own.merged, own.act, own.low_taps, own.narrow,
+        own.wide_zero, own.wide_one, own.boxes,
+    )
+    attn_backward(
+        leaving[2], me, own.grad_attn, own.res_out, own.normed, own.qkv, own.probs, own.mixed,
+        own.kern_qkv, own.kern_proj, own.attn_stats, own.attn_gains,
+        own.grad_res, sent[2], own.block_out.at[0:ATTN_ROWS],
+        own.grad_qkv, own.grad_mixed, own.grad_act, own.grad_low,
+    )
+    res_backward(
+        leaving[1], me, own.grad_res, own.down, own.inner, own.act_one, own.act_two, own.kern_first, own.kern_second,
+        own.dense_two, own.hidden_pre, own.res_stats, own.res_gains, embed,
+        own.grad_attn, sent[1], own.stage,
+        own.wide, own.grad_act,
+    )
+    stem_backward(
+        leaving[0], me, noisy, own.top, own.skip, own.grad_attn, own.kern_down, sent[0], own.block_out,
+        own.taps, stem_wide, stem_wide_zero, own.wide_one.at[:, :, 0 : 2 * C2], own.act,
+    )
+
+
+def local_step(me, arrays, places, shapes, out_places, noisy, clean, factor, embed):
+    def body(me, arrays, noisy, clean, factor, embed, loss, sent, *refs):
+        gathered = [[arrays[place[0]] for place in block] for block in places]
+        leaving = [[sent[place[0]] for place in block] for block in out_places]
+        rest = [[place[1:] for place in block] for block in places]
+        out_rest = [[place[1:] for place in block] for block in out_places]
+        whole_step(rest, out_rest, me, gathered, noisy, clean, factor, embed, loss, leaving, *refs)
+
     return run(
-        partial(stem_forward, places),
-        [me, arrays, noisy],
-        [sds((4, ROWS, C1)), sds((ROWS, C2)), sds((9 * C1, C2), bf16)],
-        [
-            pltpu.VMEM((STEM_ROWS, LANES), f32), pltpu.VMEM((72, 4 * ROWS), f32),
-            wide_scratch(3 * C1), wide_scratch(3 * C1),
-        ],
-    )
-
-
-def forward_res(me, weights, down, embed):
-    arrays, places = weights
-    return run(
-        partial(res_forward, places),
-        [me, arrays, down, embed],
-        [
-            sds((ROWS, C2)), sds((ROWS, C2)), sds((ROWS, C2), bf16), sds((ROWS, C2), bf16),
-            sds((9 * C2, C2), bf16), sds((9 * C2, C2), bf16), sds((TEMB, C2), bf16), sds((8, TEMB)),
-            sds((16, C2)), sds((8, C2)),
-        ],
-        [pltpu.VMEM((RES_ROWS, LANES), f32), pltpu.VMEM((TDIM, TEMB), bf16), wide_scratch(3 * C2)],
-    )
-
-
-def forward_attn(me, weights, res_out):
-    arrays, places = weights
-    return run(
-        partial(attn_forward, places),
-        [me, arrays, res_out],
-        [
-            sds((ROWS, C2), bf16), sds((ROWS, C2), bf16), sds((ROWS, 3 * C2), bf16), sds((IMGS, LOW, LOW)),
-            sds((ROWS, C2), bf16), sds((C2, 3 * C2), bf16), sds((C2, C2), bf16), sds((8, C2)), sds((8, C2)),
-        ],
-        [pltpu.VMEM((ATTN_ROWS, LANES), f32)],
-    )
-
-
-def both_head(me, weights, leaving, attn_low, top, clean, factor):
-    arrays, places = weights
-    shapes, out_places = leaving
-    return run(
-        partial(head_step, places, out_places),
-        [me, arrays, attn_low, top, clean, factor],
-        [sds((ROWS, C2)), sds((4, ROWS, C1)), sds((1, 1)), shapes],
-        [
-            pltpu.VMEM((HEAD_ROWS, LANES), f32),
-            pltpu.VMEM((HEAD_ROWS, LANES), f32), wide_scratch(3 * C2), pltpu.VMEM((2, 6 * C2, C2), bf16),
-            pltpu.VMEM((4, ROWS, C1), f32), pltpu.VMEM((4, ROWS, C1), bf16), pltpu.VMEM((72, 4 * ROWS), f32),
-            pltpu.VMEM((72, LANES), f32), wide_scratch(3 * C2), wide_scratch(3 * C2), wide_scratch(6 * C1, f32),
-        ],
-    )
-
-
-def backward_attn(me, leaving, *saved):
-    shapes, out_places = leaving
-    return run(
-        partial(attn_backward, out_places),
-        [me, *saved],
-        [sds((ROWS, C2)), shapes],
-        [
-            pltpu.VMEM((ATTN_ROWS, LANES), f32),
-            pltpu.VMEM((ROWS, 3 * C2), bf16), pltpu.VMEM((ROWS, C2), bf16), pltpu.VMEM((ROWS, C2), f32),
-            pltpu.VMEM((ROWS, C2), bf16),
-        ],
-    )
-
-
-def backward_res(me, leaving, *saved):
-    shapes, out_places = leaving
-    return run(
-        partial(res_backward, out_places),
-        [me, *saved],
-        [sds((ROWS, C2)), shapes],
-        [pltpu.VMEM((RES_ROWS, LANES), f32), wide_scratch(3 * C2), pltpu.VMEM((ROWS, C2), f32)],
-    )
-
-
-def backward_stem(me, leaving, *saved):
-    shapes, out_places = leaving
-    return run(
-        partial(stem_backward, out_places),
-        [me, *saved],
-        [shapes],
-        [
-            pltpu.VMEM((STEM_ROWS, LANES), f32),
-            pltpu.VMEM((72, 4 * ROWS), f32), wide_scratch(3 * C1), wide_scratch(3 * C1), wide_scratch(2 * C2),
-            pltpu.VMEM((4, ROWS, C1), bf16),
-        ],
+        body,
+        [me, arrays, noisy, clean, factor, embed],
+        [sds((1, 1)), shapes],
+        [pltpu.VMEM(shape, dtype) for shape, dtype in SAVED.values()],
     )
 
 
@@ -947,11 +927,11 @@
     return jnp.pad(split, ((0, 8 - CIN), (0, 0)))
 
 
-def prepare(clean_images, noise_field, step_counts, time_index, teacher_size, image_count, total_live):
+def prepare(clean_images, noise_field, step_counts, time_index, teacher_size, image_count):
     slot_count = clean_images.shape[0]
     time_values, alpha_t, sigma_t, weight = plan(step_counts, time_index, teacher_size)
     live_mask = (jnp.arange(slot_count, dtype=jnp.int32) < image_count).astype(f32)
-    factor = live_mask * weight / total_live
+    factor = live_mask * weight
     noisy = (alpha_t[:, None, None] * clean_images + sigma_t[:, None, None] * noise_field).astype(bf16).astype(f32)
     embed = jnp.pad(sinusoid(time_values), ((0, 8 - IMGS), (0, 0)))
     factor_lanes = jnp.repeat(factor, LOW)[None, :]
@@ -959,113 +939,110 @@
 
 
 AXES = ("dp", "fsdp")
+BLOCK_ROWS = (STEM_ROWS, RES_ROWS, ATTN_ROWS, HEAD_ROWS)
+SHARD_ROWS = (80, 344, 72, 80)
+SPAN = 32
+HALVES = (
+    (((0, 0, 80), (1, 0, 200)), (2, 4)),
+    (((1, 200, 344), (3, 0, 80), (2, 0, 72)), (4, 2)),
+)
+HALF_ROWS = tuple(sum(hi - lo for _, lo, hi in members) for members, _ in HALVES)
+LINE = (0, 8, 16, 24)
 
 
 def swap(values, mask):
-    count = lax.axis_size(AXES)
-    return lax.ppermute(values, AXES, [(here, here ^ mask) for here in range(count)])
-
-
-def axis_rounds(count, swapped):
-    bits = [1 << at for at in range(1, count.bit_length() - 1)]
-    plane = bits[:2][::-1] if swapped else bits[:2]
-    rest = bits[2:]
-    return [[bit] for bit in plane], [rest[at : at + 2] for at in range(0, len(rest), 2)]
-
-
-def spans(bits):
-    return [sum(bit for place, bit in enumerate(bits) if number >> place & 1) for number in range(1 << len(bits))]
-
-
-def gather(shard, swapped):
-    count = lax.axis_size(AXES)
-    plane, rest = axis_rounds(count, swapped)
-    held, masks = shard[None], [0]
-    for bits in rest + plane[::-1]:
-        reach = spans(bits)[1:]
-        arrived = [swap(held, mask) for mask in reach]
-        held = jnp.concatenate([held] + arrived, axis=0)
-        masks = masks + [mask ^ own for mask in reach for own in masks]
-    return [held, swap(held, 1)], [masks, [mask ^ 1 for mask in masks]]
-
-
-def reduce_masks(count, swapped):
-    plane, rest = axis_rounds(count, swapped)
-    order = [0]
-    for bits in (rest[::-1] + plane[::-1]):
-        order = [mask ^ own for mask in spans(bits) for own in order]
-    return order
-
-
-def reduce(kept, sent, swapped):
-    count = lax.axis_size(AXES)
-    plane, rest = axis_rounds(count, swapped)
-    total = kept.astype(f32) + swap(sent, 1).astype(f32)
-    for bits in plane + rest:
-        reach = spans(bits)
-        size = total.shape[0] // len(reach)
-        arrived = [swap(total[size * at : size * (at + 1)].astype(bf16), mask) for at, mask in enumerate(reach) if at]
-        total = total[:size]
-        for piece in arrived:
-            total = total + piece.astype(f32)
-    return total[0]
-
-
-BLOCK_ROWS = (STEM_ROWS, RES_ROWS, ATTN_ROWS, HEAD_ROWS)
-GATHERS = (
-    (((0, 0, 80), (1, 0, 200)), False),
-    (((1, 200, 344), (3, 0, 80), (2, 0, 72)), True),
-)
-REDUCES = (
-    ((0, 80, False),),
-    ((0, 176, False), (176, 344, True)),
-    ((0, 72, True),),
-    ((0, 80, False),),
-)
-
-
-def ordered_weights(shards):
-    found = []
-    for shard, rows in zip(shards, BLOCK_ROWS):
-        whole = lax.all_gather(shard.reshape(-1), AXES, axis=0, tiled=True).reshape(1, rows, LANES)
-        found.append(([whole], [([0], 0, rows, 0, 0)]))
+    return lax.ppermute(values, AXES, [(here, here ^ mask) for here in range(SPAN)])
+
+
+def half_places(number, array, masks):
+    at, found = 0, []
+    for block, lo, hi in HALVES[number][0]:
+        found.append((block, (array, masks, at, at + hi - lo, SHARD_ROWS[block], lo)))
+        at += hi - lo
     return found
 
 
-def gathered_weights(shards):
-    found = [([], []) for _ in shards]
-    for members, swapped in GATHERS:
-        group = jnp.concatenate([shards[block][lo:hi] for block, lo, hi in members], axis=0)
-        arrays, masks = gather(group, swapped)
-        at = 0
+def gather_halves(shards):
+    own = jnp.concatenate(
+        [shards[block][lo:hi] for members, _ in HALVES for block, lo, hi in members], axis=0
+    )
+    line = [own] + [swap(own, mask) for mask in LINE[1:]]
+    arrays, places = [], [[] for _ in shards]
+
+    def add(number, array, masks):
+        for block, place in half_places(number, len(arrays), masks):
+            places[block].append(place)
+        arrays.append(array)
+
+    held = []
+    for number, (_, (last, first)) in enumerate(HALVES):
+        begin = number * HALF_ROWS[0]
+        near = jnp.stack([piece[begin : begin + HALF_ROWS[number]] for piece in line], axis=0)
+        held.append(jnp.concatenate([near, swap(near, first)], axis=0))
+    for number, (_, (last, first)) in enumerate(HALVES):
+        masks = [a ^ b for a in (0, first) for b in LINE]
+        far = swap(held[number], last)
+        add(number, held[number], masks)
+        add(number, far, [mask ^ last for mask in masks])
+        add(number, swap(held[number], 1), [mask ^ 1 for mask in masks])
+        add(number, swap(far, 1), [mask ^ last ^ 1 for mask in masks])
+    return arrays, places
+
+
+def leaving_halves():
+    shapes, places = [], [[] for _ in SHARD_ROWS]
+    for number, (_, (first, last)) in enumerate(HALVES):
+        for core in (0, 1):
+            for side in (0, first):
+                masks = [core ^ side ^ a ^ b for a in (0, last) for b in LINE]
+                for block, place in half_places(number, len(shapes), masks):
+                    places[block].append(place)
+                shapes.append(sds((8, HALF_ROWS[number], LANES), bf16))
+    return shapes, places
+
+
+def reduce_halves(leaving):
+    totals = []
+    crossed = [[None, None], [None, None]]
+    for side in (1, 0):
+        for number in (0, 1):
+            kept, sent = leaving[4 * number + side], leaving[4 * number + 2 + side]
+            crossed[number][side] = kept.astype(f32) + swap(sent, 1).astype(f32)
+    for number, (_, (first, last)) in enumerate(HALVES):
+        near, far = crossed[number]
+        totals.append(near + swap(far.astype(bf16), first).astype(f32))
+    for number, (_, (first, last)) in enumerate(HALVES):
+        total = totals[number]
+        totals[number] = total[:4] + swap(total[4:].astype(bf16), last).astype(f32)
+    whole = jnp.concatenate(totals, axis=1)
+    result = whole[0]
+    for number, mask in enumerate(LINE[1:]):
+        result = result + swap(whole[number + 1].astype(bf16), mask).astype(f32)
+    pieces, at = [[] for _ in SHARD_ROWS], 0
+    for members, _ in HALVES:
         for block, lo, hi in members:
-            for array, owners in zip(arrays, masks):
-                found[block][0].append(array)
-                found[block][1].append((owners, at, at + hi - lo, shards[block].shape[0], lo))
+            pieces[block].append(result[at : at + hi - lo])
             at += hi - lo
-    return found
-
-
-def leaving_shapes(block, count, ordered):
-    rows = BLOCK_ROWS[block]
-    if ordered:
-        return [sds((1, rows, LANES))], [([0], 0, rows, 0, 0)]
-    shapes, places = [], []
-    for lo, hi, swapped in REDUCES[block]:
-        masks = reduce_masks(count, swapped)
-        for core in (0, 1):
-            shapes.append(sds((count // 2, hi - lo, LANES), bf16))
-            places.append(([mask ^ core for mask in masks], 0, hi - lo, rows // count, lo))
-    return shapes, places
-
-
-def reduced(block, leaving, ordered):
-    if ordered:
-        return lax.psum_scatter(leaving[0].reshape(-1), AXES, scatter_dimension=0, tiled=True)
-    parts = []
-    for number, (lo, hi, swapped) in enumerate(REDUCES[block]):
-        parts.append(reduce(leaving[2 * number], leaving[2 * number + 1], swapped))
-    return jnp.concatenate(parts, axis=0).reshape(-1)
+    return [jnp.concatenate(piece, axis=0).reshape(-1) for piece in pieces]
+
+
+def gather_whole(shards):
+    arrays = [
+        lax.all_gather(shard.reshape(-1), AXES, axis=0, tiled=True).reshape(1, rows, LANES)
+        for shard, rows in zip(shards, BLOCK_ROWS)
+    ]
+    return arrays, [[(block, (0,), 0, rows, 0, 0)] for block, rows in enumerate(BLOCK_ROWS)]
+
+
+def leaving_whole():
+    shapes = [sds((1, rows, LANES), bf16) for rows in BLOCK_ROWS]
+    return shapes, [[(block, (0,), 0, rows, 0, 0)] for block, rows in enumerate(BLOCK_ROWS)]
+
+
+def reduce_whole(leaving):
+    return [
+        lax.psum_scatter(array.astype(f32).reshape(-1), AXES, scatter_dimension=0, tiled=True) for array in leaving
+    ]
 
 
 def scalar_sums(values):
@@ -1096,41 +1073,21 @@
     masters = (stem_master, res_master, attn_master, head_master)
     firsts = (stem_first, res_first, attn_first, head_first)
     seconds = (stem_second, res_second, attn_second, head_second)
-    count = lax.axis_size(AXES)
-    ordered = count != 32
     me = lax.axis_index(AXES).astype(jnp.int32).reshape(1)
     shards = [master.astype(bf16).reshape(-1, LANES) for master in masters]
-    weights = ordered_weights(shards) if ordered else gathered_weights(shards)
-    leaving = [leaving_shapes(block, count, ordered) for block in range(4)]
-    (total_live,) = scalar_sums([image_counts[0].astype(f32)])
+    laid_out = lax.axis_size(AXES) == SPAN and tuple(shard.shape[0] for shard in shards) == SHARD_ROWS
+    arrays, places = gather_halves(shards) if laid_out else gather_whole(shards)
+    shapes, out_places = leaving_halves() if laid_out else leaving_whole()
     noisy, clean, factor, embed = prepare(
-        clean_images, noise_field, step_counts, time_index, teacher_size, image_counts[0], total_live
-    )
-    top, down, kern_down = forward_stem(me, weights[0], noisy)
-    inner, res_out, act_one, act_two, kern_first, kern_second, dense_two, hidden_pre, stats, gains = forward_res(
-        me, weights[1], down, embed
-    )
-    attn_low, normed, qkv, probs, mixed, kern_qkv, kern_proj, attn_stats, attn_gains = forward_attn(
-        me, weights[2], res_out
-    )
-    grad_attn, skip, loss_local, head_out = both_head(
-        me, weights[3], leaving[3], attn_low, top, clean, factor
-    )
-    grad_res, attn_out = backward_attn(
-        me, leaving[2], grad_attn, res_out, normed, qkv, probs, mixed, kern_qkv, kern_proj, attn_stats, attn_gains
-    )
-    grad_down, res_out_grads = backward_res(
-        me, leaving[1], grad_res, down, inner, act_one, act_two, kern_first, kern_second, dense_two, hidden_pre,
-        stats, gains, embed,
-    )
-    (stem_out,) = backward_stem(me, leaving[0], noisy, top, skip, grad_down, kern_down)
-    shard_grads = [
-        reduced(block, out, ordered) for block, out in enumerate((stem_out, res_out_grads, attn_out, head_out))
-    ]
+        clean_images, noise_field, step_counts, time_index, teacher_size, image_counts[0]
+    )
+    loss_local, leaving = local_step(me, arrays, places, shapes, out_places, noisy, clean, factor, embed)
+    shard_grads = reduce_halves(leaving) if laid_out else reduce_whole(leaving)
     sum_local = sum((jnp.sum(jnp.square(gradient)) for gradient in shard_grads))
-    loss_value, sum_sq = scalar_sums([loss_local, sum_local])
-    grad_norm = jnp.sqrt(sum_sq)
-    clip_scale = clip_limit / jnp.maximum(grad_norm, clip_limit)
+    loss_sum, sum_sq, total_live = scalar_sums([loss_local, sum_local, image_counts[0].astype(f32)])
+    loss_value = loss_sum / total_live
+    grad_norm = jnp.sqrt(sum_sq) / total_live
+    clip_scale = clip_limit / jnp.maximum(grad_norm, clip_limit) / total_live
     step_value = adam_step[0].astype(f32)
     results = [loss_value, grad_norm]
     for block_idx in range(4):

time: 210 us -> 171 us (0.81); the launches traced: 209 us -> 168 us
  starting transfers between devices: 61.4 us -> 30.4 us
  Pallas kernels: 70.5 us -> 43.6 us
  waiting for transfers between devices: 41.2 us -> 58.7 us
  local copies, waits for them, and re-layouts: 17.5 us -> 10.3 us
  between operations: 7.17 us -> 11.2 us
    ppermute x42 -> x22, starting transfers between devices: 55 us -> 25.4 us  [swap(): lax.ppermute(values, AXES, [(here, here ^ mask) for here in range(SPAN)])]
    pallas_call x7 -> x1, Pallas kernels: 70.5 us -> 43.6 us  [run(): pl.pallas_call(kernel, out_shape=out_leaves, in_specs=[pl.BlockSpec(memor...]
    ppermute x42 -> x22, waiting for transfers between devices: 34.8 us -> 52.4 us  [swap(): lax.ppermute(values, AXES, [(here, here ^ mask) for here in range(SPAN)])]
    concatenate x5 -> x2, local copies, waits for them, and re-layouts: 4.66 us -> 0.77 us  [gather_halves(): held.append(jnp.concatenate([near, swap(near, first)], axis=0))]
    unnamed x55 -> x47, local copies, waits for them, and re-layouts: 6.64 us -> 3.23 us
    reshape x3 -> x0, other arithmetic: 2.34 us -> none  [per_device(): shards = [master.astype(bf16).reshape(-1, LANES) for master in masters]]
    all_to_all x2 -> x1, starting transfers between devices: 6.33 us -> 5.04 us  [scalar_sums(): arrived = lax.all_to_all(sent, AXES, 0, 0, tiled=True)]
    all_to_all x2 -> x1, waiting for transfers between devices: 6.34 us -> 6.34 us  [scalar_sums(): arrived = lax.all_to_all(sent, AXES, 0, 0, tiled=True)]
  transfers between devices with their start and end apart: 44 -> 23, of which waited for: 16 -> 13; matrix products, arithmetic and copies ran while one was open for 9% -> 8% of each run, Pallas kernels for 12% -> 0%
where the time goes in v1:
time: 171 us; the launch traced here: 168 us
  waiting for transfers between devices  58.7 us (34%)
  Pallas kernels  43.6 us (25%)
  starting transfers between devices  30.4 us (18%)
  other arithmetic  13.4 us (8%)
  between operations  11.2 us (7%)
  local copies, waits for them, and re-layouts  10.3 us (6%)
    ppermute x22, waiting for transfers between devices, swap(): lax.ppermute(values, AXES, [(here, here ^ mask) for here in range(SPAN)])  52.4 us
    pallas_call x1, Pallas kernels, run(): pl.pallas_call(kernel, out_shape=out_leaves, in_specs=[pl.BlockSpec(memor...  43.6 us
    ppermute x22, starting transfers between devices, swap(): lax.ppermute(values, AXES, [(here, here ^ mask) for here in range(SPAN)])  25.4 us
    all_to_all x1, waiting for transfers between devices, scalar_sums(): arrived = lax.all_to_all(sent, AXES, 0, 0, tiled=True)  6.34 us
    all_to_all x1, starting transfers between devices, scalar_sums(): arrived = lax.all_to_all(sent, AXES, 0, 0, tiled=True)  5.04 us
  transfers between devices with their start and end apart: 23, of which 13 were waited for; matrix products, arithmetic and copies ran while one was open for 8% of the time, Pallas kernels for 0%

profile of v1, /device:TPU:0, one launch (start us, length us, event | category | flops | bytes accessed | tf_op | source)
XLA Modules:
  0.0 167.6 jit_solution(7914755000453935298)
XLA Ops:
  0.7 0.9 convert_element_type.113
  1.6 0.8 constant_dynamic-update-slice_fusion.4
  2.4 0.8 constant_dynamic-update-slice_fusion.1
  3.2 0.8 constant_dynamic-update-slice_fusion
  4.0 3.1 %collective-permute-start = (bf16[576,128]{1,0:T(8,128)(2,1)S(1)}, bf16[576,128]{1,0:T(8,128)(2,1)S(1)}, u32[]{:S(2)}, u32[]{:S(2)}) collective-permute-start(bf16[576,128]{1,0:T(8,128)(2,1)S(1)} %get-tuple-element.56), channel_id=1, source_target_pairs={{0,8},{1,9},{2,10},{3,11},{4,12},{5,13},{6,14},{7,15},{8,0},{9,1},... | collective-permute-start | bytes 442376 | tf_op jit(solution)/shard_map/ppermute | solution.py:954
  7.1 2.6 %collective-permute-start.1 = (bf16[576,128]{1,0:T(8,128)(2,1)S(1)}, bf16[576,128]{1,0:T(8,128)(2,1)S(1)}, u32[]{:S(2)}, u32[]{:S(2)}) collective-permute-start(bf16[576,128]{1,0:T(8,128)(2,1)S(1)} %get-tuple-element.56), channel_id=1, source_target_pairs={{0,16},{1,17},{2,18},{3,19},{4,20},{5,21},{6,22},{7,23},{8,24},{9,... | collective-permute-start | bytes 442376 | tf_op jit(solution)/shard_map/ppermute | solution.py:954
  9.7 0.8 broadcast_multiply_fusion
  10.5 0.6 constant_dynamic-update-slice_fusion.9
  11.8 7.7 %collective-permute-done.2 = bf16[576,128]{1,0:T(8,128)(2,1)S(1)} collective-permute-done((bf16[576,128]{1,0:T(8,128)(2,1)S(1)}, bf16[576,128]{1,0:T(8,128)(2,1)S(1)}, u32[]{:S(2)}, u32[]{:S(2)}) %collective-permute-start.2) | collective-permute-done | bytes 147488 | tf_op jit(solution)/shard_map/ppermute | solution.py:954
  19.5 1.5 collective-permute-done.1
  21.2 1.6 collective-permute-start.7
  22.8 1.6 collective-permute-start.3
  24.5 0.6 constant_dynamic-update-slice_fusion.8
  25.1 0.6 constant_dynamic-update-slice_fusion.7
  25.7 0.6 constant_dynamic-update-slice_fusion.6
  26.4 3.4 %collective-permute-done.3 = bf16[4,280,128]{2,1,0:T(8,128)(2,1)S(1)} collective-permute-done((bf16[4,280,128]{2,1,0:T(8,128)(2,1)S(1)}, bf16[4,280,128]{2,1,0:T(8,128)(2,1)S(1)}, u32[]{:S(2)}, u32[]{:S(2)}) %collective-permute-start.3) | collective-permute-done | bytes 286752 | tf_op jit(solution)/shard_map/ppermute | solution.py:954
  29.7 0.7 constant_dynamic-update-slice_fusion.5.refs_1_
  30.8 1.6 collective-permute-start.8
  33.3 8.4 %collective-permute-done.4.refs_2_ = bf16[8,280,128]{2,1,0:T(8,128)(2,1)} collective-permute-done((bf16[8,280,128]{2,1,0:T(8,128)(2,1)}, bf16[8,280,128]{2,1,0:T(8,128)(2,1)}, u32[]{:S(2)}, u32[]{:S(2)}) %collective-permute-start.4) | collective-permute-done | bytes 573472 | tf_op jit(solution)/shard_map/ppermute | solution.py:954
  41.7 0.9 collective-permute-done.8.refs_6_
  43.6 1.6 copy.48
  46.1 1.7 %copy.50 = f32[3,2,2,4,16,16]{5,4,3,2,1,0:T(8,128)S(1)} copy(f32[3,2,2,4,16,16]{3,2,5,1,4,0:T(2,128)S(1)} %bitcast.118) | data formatting | bytes 98304 | tf_op jit(solution)/shard_map/transpose | solution.py:926
  48.1 0.7 pad.15.refs_10_
  48.7 0.7 select_maximum_fusion.refs_12_
  49.4 0.7 pad_convert_fusion.refs_9_
  50.1 43.6 %shard_map.322 = (f32[1,1]{1,0:T(1,128)}, bf16[8,280,128]{2,1,0:T(8,128)(2,1)}, bf16[8,280,128]{2,1,0:T(8,128)(2,1)}, bf16[8,280,128]{2,1,0:T(8,128)(2,1)}, bf16...) custom-call(s32[1]{0:T(128)} %bitcast.refs_0_, ...), custom_call_target="tpu_custom_call" | custom-call | tf_op jit(solution)/shard_map/pallas_call | solution.py:812
  94.9 1.2 collective-permute-done.12
  96.1 1.2 add_convert_fusion.1
  97.3 1.5 collective-permute-start.13
  99.0 1.6 collective-permute-start.17
  100.6 12.0 %collective-permute-done.13 = bf16[8,280,128]{2,1,0:T(8,128)(2,1)S(1)} collective-permute-done((bf16[8,280,128]{2,1,0:T(8,128)(2,1)S(1)}, bf16[8,280,128]{2,1,0:T(8,128)(2,1)S(1)}, u32[]{:S(2)}, u32[]{:S(2)}) %collective-permute-start.13) | collective-permute-done | bytes 573472 | tf_op jit(solution)/shard_map/ppermute | solution.py:954
  112.9 1.6 collective-permute-start.14
  115.0 1.2 collective-permute-start.18
  116.3 5.0 %collective-permute-done.14 = bf16[4,280,128]{2,1,0:T(8,128)(2,1)S(1)} collective-permute-done((bf16[4,280,128]{2,1,0:T(8,128)(2,1)S(1)}, bf16[4,280,128]{2,1,0:T(8,128)(2,1)S(1)}, u32[]{:S(2)}, u32[]{:S(2)}) %collective-permute-start.14) | collective-permute-done | bytes 286752 | tf_op jit(solution)/shard_map/ppermute | solution.py:954
  121.3 2.1 %collective-permute-done.18 = bf16[4,296,128]{2,1,0:T(8,128)(2,1)S(1)} collective-permute-done((bf16[4,296,128]{2,1,0:T(8,128)(2,1)S(1)}, bf16[4,296,128]{2,1,0:T(8,128)(2,1)S(1)}, u32[]{:S(2)}, u32[]{:S(2)}) %collective-permute-start.18) | collective-permute-done | bytes 303136 | tf_op jit(solution)/shard_map/ppermute | solution.py:954
  123.7 4.1 %collective-permute-start.19 = (bf16[576,128]{1,0:T(8,128)(2,1)S(1)}, bf16[576,128]{1,0:T(8,128)(2,1)S(1)}, u32[]{:S(2)}, u32[]{:S(2)}) collective-permute-start(bf16[576,128]{1,0:T(8,128)(2,1)S(1)} %get-tuple-element.62), channel_id=1, source_target_pairs={{0,8},{1,9},{2,10},{3,11},{4,12},{5,13},{6,14},{7,15},{8,0},{9,1},... | collective-permute-start | bytes 442376 | tf_op jit(solution)/shard_map/ppermute | solution.py:954
  127.8 1.5 collective-permute-start.20
  129.2 1.4 collective-permute-start.21
  130.6 1.9 %collective-permute-done.19 = bf16[576,128]{1,0:T(8,128)(2,1)S(1)} collective-permute-done((bf16[576,128]{1,0:T(8,128)(2,1)S(1)}, bf16[576,128]{1,0:T(8,128)(2,1)S(1)}, u32[]{:S(2)}, u32[]{:S(2)}) %collective-permute-start.19) | collective-permute-done | bytes 147488 | tf_op jit(solution)/shard_map/ppermute | solution.py:954
  132.5 8.0 %collective-permute-done.20 = bf16[576,128]{1,0:T(8,128)(2,1)S(1)} collective-permute-done((bf16[576,128]{1,0:T(8,128)(2,1)S(1)}, bf16[576,128]{1,0:T(8,128)(2,1)S(1)}, u32[]{:S(2)}, u32[]{:S(2)}) %collective-permute-start.20) | collective-permute-done | bytes 147488 | tf_op jit(solution)/shard_map/ppermute | solution.py:954
  141.2 0.6 multiply_reduce_fusion
  145.1 0.7 pad_maximum_fusion.3
  145.8 0.6 broadcast_in_dim.8
  146.4 5.0 %all-to-all-start = ((f32[32,1,128]{2,1,0:T(1,128)}), f32[32,1,128]{2,1,0:T(1,128)S(1)}, u32[]{:S(2)}, u32[]{:S(2)}) async-start(f32[32,1,128]{2,1,0:T(1,128)} %broadcast_in_dim.8), calls=%async_computation | async-start | bytes 32768 | tf_op jit(solution)/shard_map/all_to_all | solution.py:1052
  152.2 6.3 %all-to-all-done = f32[32,1,128]{2,1,0:T(1,128)S(1)} async-done(((f32[32,1,128]{2,1,0:T(1,128)}), f32[32,1,128]{2,1,0:T(1,128)S(1)}, u32[]{:S(2)}, u32[]{:S(2)}) %all-to-all-start) | async-done | bytes 16416 | tf_op jit(solution)/shard_map/all_to_all | solution.py:1052
  162.6 0.7 fusion.17
  163.3 0.9 fusion.20
  164.2 0.7 fusion.14
  (101 shorter events, 7.8 us)
Async XLA Ops:
  4.0 17.1 %collective-permute-start = (bf16[576,128]{1,0:T(8,128)(2,1)S(1)}, bf16[576,128]{1,0:T(8,128)(2,1)S(1)}, u32[]{:S(2)}, u32[]{:S(2)}) collective-permute-start(bf16[576,128]{1,0:T(8,128)(2,1)S(1)} %get-tuple-element.56), channel_id=1, source_target_pairs={{0,8},{1,9},{2,10},{3,11},{4,12},{5,13},{6,14},{7,15},{8,0},{9,1},... | collective-permute-start | bytes 442376 | tf_op jit(solution)/shard_map/ppermute | solution.py:954
  7.1 14.0 %collective-permute-start.1 = (bf16[576,128]{1,0:T(8,128)(2,1)S(1)}, bf16[576,128]{1,0:T(8,128)(2,1)S(1)}, u32[]{:S(2)}, u32[]{:S(2)}) collective-permute-start(bf16[576,128]{1,0:T(8,128)(2,1)S(1)} %get-tuple-element.56), channel_id=1, source_target_pairs={{0,16},{1,17},{2,18},{3,19},{4,20},{5,21},{6,22},{7,23},{8,24},{9,... | collective-permute-start | bytes 442376 | tf_op jit(solution)/shard_map/ppermute | solution.py:954
  9.7 9.9 %collective-permute-start.2 = (bf16[576,128]{1,0:T(8,128)(2,1)S(1)}, bf16[576,128]{1,0:T(8,128)(2,1)S(1)}, u32[]{:S(2)}, u32[]{:S(2)}) collective-permute-start(bf16[576,128]{1,0:T(8,128)(2,1)S(1)} %get-tuple-element.56), channel_id=1, source_target_pairs={{0,24},{1,25},{2,26},{3,27},{4,28},{5,29},{6,30},{7,31},{8,16},{9,... | collective-permute-start | bytes 442376 | tf_op jit(solution)/shard_map/ppermute | solution.py:954
  21.2 9.6 %collective-permute-start.7 = (bf16[4,296,128]{2,1,0:T(8,128)(2,1)S(1)}, bf16[4,296,128]{2,1,0:T(8,128)(2,1)S(1)}, u32[]{:S(2)}, u32[]{:S(2)}) collective-permute-start(bf16[4,296,128]{2,1,0:T(8,128)(2,1)S(1)} %pad_maximum_fusion.1), channel_id=1, source_target_pairs={{0,2},{1,3},{2,0},{3,1},{4,6},{5,7},{6,4},{7,5},{8,10},{9,11},{10,... | collective-permute-start | bytes 909320 | tf_op jit(solution)/shard_map/ppermute | solution.py:954
  22.8 9.8 %copy-start.5 = (f32[4,3,1024]{2,0,1:T(4,128)S(1)}, f32[4,3,1024]{2,0,1:T(4,128)}, u32[]{:S(2)}) copy-start(f32[4,3,1024]{2,0,1:T(4,128)} %param.19) | copy-start | bytes 147460
  22.8 9.8 %copy-start.11 = (f32[4,3,1024]{2,0,1:T(4,128)S(1)}, f32[4,3,1024]{2,0,1:T(4,128)}, u32[]{:S(2)}) copy-start(f32[4,3,1024]{2,0,1:T(4,128)} %param.20) | copy-start | bytes 147460
  22.8 6.9 %collective-permute-start.3 = (bf16[4,280,128]{2,1,0:T(8,128)(2,1)S(1)}, bf16[4,280,128]{2,1,0:T(8,128)(2,1)S(1)}, u32[]{:S(2)}, u32[]{:S(2)}) collective-permute-start(bf16[4,280,128]{2,1,0:T(8,128)(2,1)S(1)} %pad_maximum_fusion.2), channel_id=1, source_target_pairs={{0,4},{1,5},{2,6},{3,7},{4,0},{5,1},{6,2},{7,3},{8,12},{9,13},{10,... | collective-permute-start | bytes 860168 | tf_op jit(solution)/shard_map/ppermute | solution.py:954
  30.5 11.2 %collective-permute-start.4 = (bf16[8,280,128]{2,1,0:T(8,128)(2,1)}, bf16[8,280,128]{2,1,0:T(8,128)(2,1)}, u32[]{:S(2)}, u32[]{:S(2)}) collective-permute-start(bf16[8,280,128]{2,1,0:T(8,128)(2,1)} %constant_dynamic-update-slice_fusion.5.refs_1_), channel_id=1, source_target_pairs={{0,2},{1,3},{2,0},{3,1},{4,6},{5,7},{6,4},{7,5},{8,10},{9,11},{10,... | collective-permute-start | bytes 1720328 | tf_op jit(solution)/shard_map/ppermute | solution.py:954
  30.8 12.8 %copy-start = (bf16[8,296,128]{2,1,0:T(8,128)(2,1)}, bf16[8,296,128]{2,1,0:T(8,128)(2,1)S(1)}, u32[]{:S(2)}) copy-start(bf16[8,296,128]{2,1,0:T(8,128)(2,1)S(1)} %constant_dynamic-update-slice_fusion.10.refs_5_) | copy-start | bytes 1818628
  30.8 11.8 %collective-permute-start.8 = (bf16[8,296,128]{2,1,0:T(8,128)(2,1)S(1)}, bf16[8,296,128]{2,1,0:T(8,128)(2,1)}, u32[]{:S(2)}, u32[]{:S(2)}) collective-permute-start(bf16[8,296,128]{2,1,0:T(8,128)(2,1)S(1)} %constant_dynamic-update-slice_fusion.10.refs_5_), channel_id=1, source_target_pairs={{0,4},{1,5},{2,6},{3,7},{4,0},{5,1},{6,2},{7,3},{8,12},{9,13},{10,... | collective-permute-start | bytes 1818632 | tf_op jit(solution)/shard_map/ppermute | solution.py:954
  32.7 17.4 %collective-permute-start.5 = (bf16[8,280,128]{2,1,0:T(8,128)(2,1)}, bf16[8,280,128]{2,1,0:T(8,128)(2,1)}, u32[]{:S(2)}, u32[]{:S(2)}) collective-permute-start(bf16[8,280,128]{2,1,0:T(8,128)(2,1)} %constant_dynamic-update-slice_fusion.5.refs_1_), channel_id=1, source_target_pairs={{0,1},{1,0},{2,3},{3,2},{4,5},{5,4},{6,7},{7,6},{8,9},{9,8},{10,11... | collective-permute-start | bytes 1720328 | tf_op jit(solution)/shard_map/ppermute | solution.py:954
  32.8 17.3 %collective-permute-start.9 = (bf16[8,296,128]{2,1,0:T(8,128)(2,1)S(1)}, bf16[8,296,128]{2,1,0:T(8,128)(2,1)}, u32[]{:S(2)}, u32[]{:S(2)}) collective-permute-start(bf16[8,296,128]{2,1,0:T(8,128)(2,1)S(1)} %constant_dynamic-update-slice_fusion.10.refs_5_), channel_id=1, source_target_pairs={{0,1},{1,0},{2,3},{3,2},{4,5},{5,4},{6,7},{7,6},{8,9},{9,8},{10,11... | collective-permute-start | bytes 1818632 | tf_op jit(solution)/shard_map/ppermute | solution.py:954
  41.7 8.4 %collective-permute-start.6 = (bf16[8,280,128]{2,1,0:T(8,128)(2,1)}, bf16[8,280,128]{2,1,0:T(8,128)(2,1)}, u32[]{:S(2)}, u32[]{:S(2)}) collective-permute-start(bf16[8,280,128]{2,1,0:T(8,128)(2,1)} %collective-permute-done.4.refs_2_), channel_id=1, source_target_pairs={{0,1},{1,0},{2,3},{3,2},{4,5},{5,4},{6,7},{7,6},{8,9},{9,8},{10,11... | collective-permute-start | bytes 1720328 | tf_op jit(solution)/shard_map/ppermute | solution.py:954
  42.6 7.5 %collective-permute-start.10 = (bf16[8,296,128]{2,1,0:T(8,128)(2,1)}, bf16[8,296,128]{2,1,0:T(8,128)(2,1)}, u32[]{:S(2)}, u32[]{:S(2)}) collective-permute-start(bf16[8,296,128]{2,1,0:T(8,128)(2,1)} %collective-permute-done.8.refs_6_), channel_id=1, source_target_pairs={{0,1},{1,0},{2,3},{3,2},{4,5},{5,4},{6,7},{7,6},{8,9},{9,8},{10,11... | collective-permute-start | bytes 1818632 | tf_op jit(solution)/shard_map/ppermute | solution.py:954
  93.7 5.2 %copy-start.2 = (bf16[8,296,128]{2,1,0:T(8,128)(2,1)S(1)}, bf16[8,296,128]{2,1,0:T(8,128)(2,1)}, u32[]{:S(2)}) copy-start(bf16[8,296,128]{2,1,0:T(8,128)(2,1)} %get-tuple-element.34) | copy-start | bytes 1818628
  93.7 2.4 %collective-permute-start.12 = (bf16[8,280,128]{2,1,0:T(8,128)(2,1)}, bf16[8,280,128]{2,1,0:T(8,128)(2,1)S(1)}, u32[]{:S(2)}, u32[]{:S(2)}) collective-permute-start(bf16[8,280,128]{2,1,0:T(8,128)(2,1)} %get-tuple-element.31), channel_id=1, source_target_pairs={{0,1},{1,0},{2,3},{3,2},{4,5},{5,4},{6,7},{7,6},{8,9},{9,8},{10,11... | collective-permute-start | bytes 1720328 | tf_op jit(solution)/shard_map/ppermute | solution.py:954
  94.3 4.6 %collective-permute-start.16 = (bf16[8,296,128]{2,1,0:T(8,128)(2,1)}, bf16[8,296,128]{2,1,0:T(8,128)(2,1)S(1)}, u32[]{:S(2)}, u32[]{:S(2)}) collective-permute-start(bf16[8,296,128]{2,1,0:T(8,128)(2,1)} %get-tuple-element.35), channel_id=1, source_target_pairs={{0,1},{1,0},{2,3},{3,2},{4,5},{5,4},{6,7},{7,6},{8,9},{9,8},{10,11... | collective-permute-start | bytes 1818632 | tf_op jit(solution)/shard_map/ppermute | solution.py:954
  94.4 6.3 %collective-permute-start.11 = (bf16[8,280,128]{2,1,0:T(8,128)(2,1)}, bf16[8,280,128]{2,1,0:T(8,128)(2,1)S(1)}, u32[]{:S(2)}, u32[]{:S(2)}) collective-permute-start(bf16[8,280,128]{2,1,0:T(8,128)(2,1)} %get-tuple-element.29), channel_id=1, source_target_pairs={{0,1},{1,0},{2,3},{3,2},{4,5},{5,4},{6,7},{7,6},{8,9},{9,8},{10,11... | collective-permute-start | bytes 1720328 | tf_op jit(solution)/shard_map/ppermute | solution.py:954
  94.8 19.7 %collective-permute-start.15 = (bf16[8,296,128]{2,1,0:T(8,128)(2,1)}, bf16[8,296,128]{2,1,0:T(8,128)(2,1)S(1)}, u32[]{:S(2)}, u32[]{:S(2)}) collective-permute-start(bf16[8,296,128]{2,1,0:T(8,128)(2,1)} %get-tuple-element.33), channel_id=1, source_target_pairs={{0,1},{1,0},{2,3},{3,2},{4,5},{5,4},{6,7},{7,6},{8,9},{9,8},{10,11... | collective-permute-start | bytes 1818632 | tf_op jit(solution)/shard_map/ppermute | solution.py:954
  97.3 15.3 %copy-start.4 = (bf16[8,280,128]{2,1,0:T(8,128)(2,1)S(1)}, bf16[8,280,128]{2,1,0:T(8,128)(2,1)}, u32[]{:S(2)}) copy-start(bf16[8,280,128]{2,1,0:T(8,128)(2,1)} %get-tuple-element.28) | copy-start | bytes 1720324
  97.3 15.3 %collective-permute-start.13 = (bf16[8,280,128]{2,1,0:T(8,128)(2,1)S(1)}, bf16[8,280,128]{2,1,0:T(8,128)(2,1)S(1)}, u32[]{:S(2)}, u32[]{:S(2)}) collective-permute-start(bf16[8,280,128]{2,1,0:T(8,128)(2,1)S(1)} %add_convert_fusion.1), channel_id=1, source_target_pairs={{0,2},{1,3},{2,0},{3,1},{4,6},{5,7},{6,4},{7,5},{8,10},{9,11},{10,... | collective-permute-start | bytes 1720328 | tf_op jit(solution)/shard_map/ppermute | solution.py:954
  99.0 15.7 %collective-permute-start.17 = (bf16[8,296,128]{2,1,0:T(8,128)(2,1)S(1)}, bf16[8,296,128]{2,1,0:T(8,128)(2,1)S(1)}, u32[]{:S(2)}, u32[]{:S(2)}) collective-permute-start(bf16[8,296,128]{2,1,0:T(8,128)(2,1)S(1)} %add_convert_fusion), channel_id=1, source_target_pairs={{0,4},{1,5},{2,6},{3,7},{4,0},{5,1},{6,2},{7,3},{8,12},{9,13},{10,... | collective-permute-start | bytes 1818632 | tf_op jit(solution)/shard_map/ppermute | solution.py:954
  112.7 2.1 %copy-start.3 = (bf16[8,296,128]{2,1,0:T(8,128)(2,1)S(1)}, bf16[8,296,128]{2,1,0:T(8,128)(2,1)}, u32[]{:S(2)}) copy-start(bf16[8,296,128]{2,1,0:T(8,128)(2,1)} %get-tuple-element.32) | copy-start | bytes 1818628
  112.9 8.4 %collective-permute-start.14 = (bf16[4,280,128]{2,1,0:T(8,128)(2,1)S(1)}, bf16[4,280,128]{2,1,0:T(8,128)(2,1)S(1)}, u32[]{:S(2)}, u32[]{:S(2)}) collective-permute-start(bf16[4,280,128]{2,1,0:T(8,128)(2,1)S(1)} %slice.208), channel_id=1, source_target_pairs={{0,4},{1,5},{2,6},{3,7},{4,0},{5,1},{6,2},{7,3},{8,12},{9,13},{10,... | collective-permute-start | bytes 860168 | tf_op jit(solution)/shard_map/ppermute | solution.py:954
  115.0 8.4 %collective-permute-start.18 = (bf16[4,296,128]{2,1,0:T(8,128)(2,1)S(1)}, bf16[4,296,128]{2,1,0:T(8,128)(2,1)S(1)}, u32[]{:S(2)}, u32[]{:S(2)}) collective-permute-start(bf16[4,296,128]{2,1,0:T(8,128)(2,1)S(1)} %slice.207), channel_id=1, source_target_pairs={{0,2},{1,3},{2,0},{3,1},{4,6},{5,7},{6,4},{7,5},{8,10},{9,11},{10,... | collective-permute-start | bytes 909320 | tf_op jit(solution)/shard_map/ppermute | solution.py:954
  123.6 38.9 %copy-start.10 = (f32[9216]{0:T(1024)S(1)}, f32[9216]{0:T(1024)}, u32[]{:S(2)}) copy-start(f32[9216]{0:T(1024)} %param.32) | copy-start | bytes 110596
  123.6 38.9 %copy-start.16 = (f32[9216]{0:T(1024)S(1)}, f32[9216]{0:T(1024)}, u32[]{:S(2)}) copy-start(f32[9216]{0:T(1024)} %param.34) | copy-start | bytes 110596
  123.6 38.9 %copy-start.17 = (f32[9216]{0:T(1024)S(1)}, f32[9216]{0:T(1024)}, u32[]{:S(2)}) copy-start(f32[9216]{0:T(1024)} %param.33) | copy-start | bytes 110596
  123.7 8.9 %collective-permute-start.19 = (bf16[576,128]{1,0:T(8,128)(2,1)S(1)}, bf16[576,128]{1,0:T(8,128)(2,1)S(1)}, u32[]{:S(2)}, u32[]{:S(2)}) collective-permute-start(bf16[576,128]{1,0:T(8,128)(2,1)S(1)} %get-tuple-element.62), channel_id=1, source_target_pairs={{0,8},{1,9},{2,10},{3,11},{4,12},{5,13},{6,14},{7,15},{8,0},{9,1},... | collective-permute-start | bytes 442376 | tf_op jit(solution)/shard_map/ppermute | solution.py:954
  127.8 12.7 %collective-permute-start.20 = (bf16[576,128]{1,0:T(8,128)(2,1)S(1)}, bf16[576,128]{1,0:T(8,128)(2,1)S(1)}, u32[]{:S(2)}, u32[]{:S(2)}) collective-permute-start(bf16[576,128]{1,0:T(8,128)(2,1)S(1)} %get-tuple-element.64), channel_id=1, source_target_pairs={{0,16},{1,17},{2,18},{3,19},{4,20},{5,21},{6,22},{7,23},{8,24},{9,... | collective-permute-start | bytes 442376 | tf_op jit(solution)/shard_map/ppermute | solution.py:954
  129.2 11.2 %collective-permute-start.21 = (bf16[576,128]{1,0:T(8,128)(2,1)S(1)}, bf16[576,128]{1,0:T(8,128)(2,1)S(1)}, u32[]{:S(2)}, u32[]{:S(2)}) collective-permute-start(bf16[576,128]{1,0:T(8,128)(2,1)S(1)} %get-tuple-element.63), channel_id=1, source_target_pairs={{0,24},{1,25},{2,26},{3,27},{4,28},{5,29},{6,30},{7,31},{8,16},{9,... | collective-permute-start | bytes 442376 | tf_op jit(solution)/shard_map/ppermute | solution.py:954
  130.6 32.6 %copy-start.1 = (f32[44032]{0:T(1024)S(1)}, f32[44032]{0:T(1024)}, u32[]{:S(2)}) copy-start(f32[44032]{0:T(1024)} %param.29) | copy-start | bytes 528388
  130.6 32.6 %copy-start.6 = (f32[44032]{0:T(1024)S(1)}, f32[44032]{0:T(1024)}, u32[]{:S(2)}) copy-start(f32[44032]{0:T(1024)} %param.31) | copy-start | bytes 528388
  130.6 32.6 %copy-start.7 = (f32[44032]{0:T(1024)S(1)}, f32[44032]{0:T(1024)}, u32[]{:S(2)}) copy-start(f32[44032]{0:T(1024)} %param.30) | copy-start | bytes 528388
  140.5 23.6 %copy-start.8 = (f32[10240]{0:T(1024)S(1)}, f32[10240]{0:T(1024)}, u32[]{:S(2)}) copy-start(f32[10240]{0:T(1024)} %param.26) | copy-start | bytes 122884
  140.6 23.6 %copy-start.9 = (f32[10240]{0:T(1024)S(1)}, f32[10240]{0:T(1024)}, u32[]{:S(2)}) copy-start(f32[10240]{0:T(1024)} %param.35) | copy-start | bytes 122884
  140.6 23.6 %copy-start.12 = (f32[10240]{0:T(1024)S(1)}, f32[10240]{0:T(1024)}, u32[]{:S(2)}) copy-start(f32[10240]{0:T(1024)} %param.37) | copy-start | bytes 122884
  140.6 23.6 %copy-start.13 = (f32[10240]{0:T(1024)S(1)}, f32[10240]{0:T(1024)}, u32[]{:S(2)}) copy-start(f32[10240]{0:T(1024)} %param.36) | copy-start | bytes 122884
  140.6 23.6 %copy-start.14 = (f32[10240]{0:T(1024)S(1)}, f32[10240]{0:T(1024)}, u32[]{:S(2)}) copy-start(f32[10240]{0:T(1024)} %param.28) | copy-start | bytes 122884
  140.6 23.6 %copy-start.15 = (f32[10240]{0:T(1024)S(1)}, f32[10240]{0:T(1024)}, u32[]{:S(2)}) copy-start(f32[10240]{0:T(1024)} %param.27) | copy-start | bytes 122884
  146.4 12.1 %all-to-all-start = ((f32[32,1,128]{2,1,0:T(1,128)}), f32[32,1,128]{2,1,0:T(1,128)S(1)}, u32[]{:S(2)}, u32[]{:S(2)}) async-start(f32[32,1,128]{2,1,0:T(1,128)} %broadcast_in_dim.8), calls=%async_computation | async-start | bytes 32768 | tf_op jit(solution)/shard_map/all_to_all | solution.py:1052
